TPU v7x, 512 devices: a whole 4x4x16 slice. The times are simulated.
512 devices in a mesh: dp: 32 (over y, z_lo), tp: 16 (over z_hi, x, core).
Axes of the slice: x: 4, y: 4, z: 16 (z_hi: 2, z_lo: 8; z = z_hi * 8 + z_lo), core: 2. Of those that a mesh axis runs over, the one named last changes fastest.
Arguments:
- patches: bfloat16 [64, 576, 1024], P('dp', 'tp'), may hold values from -6 to 6
- image_slot: int32 [64], P('dp'), may hold values from 0 to 1, as said below
- trainer_blocks: int32 [16], replicated, may hold values from 0 to 15, each once
- conv_weight: bfloat16 [9216, 1024], P('dp', 'tp'), may hold values from -0.0625 to 0.0625
- proj_weight: bfloat16 [1024, 8192], P('dp', 'tp'), may hold values from -0.1875 to 0.1875
Outputs:
- vision_tokens: bfloat16 [64, 144, 8192], P('dp', None, 'tp')
Inputs may be any that keep to these rules, and one draw needn't show every extreme that they name: `image_slot`: each aligned block of 2 entries, one block for each index of dp, is a permutation of 0 to 1. `trainer_blocks`: a permutation.
All inputs are finite; a program needn't handle non-finite values.
Results may differ from a plain program's by a relative error of at most 0.005.
Values may be sent and summed in bfloat16 or wider, within the bound.
A program may use at most 64 MiB of HBM per device.

v0:
```python
import jax
import jax.numpy as jnp
from jax import lax
from jax.sharding import PartitionSpec as P

GRID = 24


def from_partner(value, axis, apart):
    return lax.ppermute(value, axis, [(i, i ^ 1 << apart) for i in range(lax.axis_size(axis))])


def holder_of(trainer_blocks, tp_count):
    positions = jnp.arange(tp_count, dtype=jnp.int32)
    onehot = (trainer_blocks[:, None] == positions[None, :]).astype(jnp.int32)
    return jnp.sum(onehot * positions[:, None], axis=0)


def relayout(conv_part, proj_part, trainer_blocks, tp_count):
    half_width = tp_count // 2
    conv_rows = conv_part.shape[0] // tp_count
    proj_rows = proj_part.shape[0] // tp_count
    conv_block = conv_part.shape[1]
    proj_block = proj_part.shape[1]
    got_conv, got_proj = (
        lax.all_to_all(
            conv_part.reshape(tp_count, conv_rows, conv_block),
            "tp",
            split_axis=0,
            concat_axis=0,
            tiled=True,
        ),
        lax.all_to_all(
            proj_part.reshape(tp_count, proj_rows, proj_block),
            "tp",
            split_axis=0,
            concat_axis=0,
            tiled=True,
        ),
    )
    holder = holder_of(trainer_blocks, tp_count)
    logic_conv = jnp.take(got_conv, holder, axis=0)
    logic_proj = jnp.take(got_proj, holder, axis=0)
    paired = (
        logic_conv.reshape(half_width, 2, conv_rows, conv_block)
        .transpose(0, 2, 1, 3)
        .reshape(half_width, conv_rows, 2 * conv_block)
    )
    spread = (
        logic_proj.reshape(2, half_width, proj_rows, proj_block)
        .transpose(1, 2, 0, 3)
        .reshape(half_width, proj_rows, 2 * proj_block)
    )
    send_conv = jnp.concatenate([paired, paired], axis=0)
    send_proj = jnp.concatenate([spread, spread], axis=0)
    new_conv, new_proj = (
        lax.all_to_all(send_conv, "tp", split_axis=0, concat_axis=0, tiled=True),
        lax.all_to_all(send_proj, "tp", split_axis=0, concat_axis=0, tiled=True),
    )
    return (
        new_conv.reshape(tp_count * conv_rows, 2 * conv_block),
        new_proj.reshape(tp_count * proj_rows, 2 * proj_block),
    )


def convolve(grid_images, conv_slab, channel_block):
    count = grid_images.shape[0]
    side = grid_images.shape[1]
    channels = grid_images.shape[3]
    width_out = conv_slab.shape[1]
    padded = jnp.pad(grid_images, ((0, 0), (1, 1), (1, 1), (0, 0)))
    total = jnp.zeros((count, side, side, width_out), jnp.float32)
    for tap in range(9):
        row_shift = tap // 3
        col_shift = tap % 3
        window = padded[:, row_shift : row_shift + side, col_shift : col_shift + side, :]
        total = total + jnp.einsum(
            "nhwc,co->nhwo",
            window,
            conv_slab[tap * channels : (tap + 1) * channels],
            preferred_element_type=jnp.float32,
        )
    residual = lax.dynamic_slice_in_dim(
        grid_images, channel_block * width_out, width_out, 3
    ).astype(jnp.float32)
    feature = residual + jax.nn.silu(total)
    half_side = side // 2
    pooled = feature.reshape(count, half_side, 2, half_side, 2, width_out).mean(axis=(2, 4))
    return pooled.reshape(count, half_side * half_side, width_out).astype(jnp.bfloat16)


def per_device(patches, image_slot, trainer_blocks, conv_weight, proj_weight):
    tp_count = lax.axis_size("tp")
    half_width = tp_count // 2
    rank_index = lax.axis_index("tp")
    which_half = rank_index // half_width
    engine_rank = rank_index % half_width
    img_local = patches.shape[0]
    img_half = img_local // 2
    channels = patches.shape[2]
    full_conv, full_proj = (
        lax.all_gather(conv_weight, "dp", axis=0, tiled=True),
        lax.all_gather(proj_weight, "dp", axis=0, tiled=True),
    )
    conv_slab, proj_slab = relayout(full_conv, full_proj, trainer_blocks, tp_count)
    gathered = lax.all_gather(patches, "tp", axis=1, tiled=True)
    chosen = lax.dynamic_slice_in_dim(image_slot, which_half * img_half, img_half, 0)
    items = jnp.take(gathered, chosen, axis=0)
    pooled = convolve(items.reshape(items.shape[0], GRID, GRID, channels), conv_slab, engine_rank)
    collected = pooled
    for bit_index in range(half_width.bit_length() - 1):
        partner = from_partner(collected, "tp", bit_index)
        upper = engine_rank >> bit_index & 1
        collected = jnp.where(
            upper == 1,
            jnp.concatenate([partner, collected], axis=2),
            jnp.concatenate([collected, partner], axis=2),
        )
    projected = jnp.einsum(
        "npc,cq->npq", collected, proj_slab, preferred_element_type=jnp.float32
    ).astype(jnp.bfloat16)
    pieces = projected.reshape(projected.shape[0], projected.shape[1], 2, projected.shape[2] // 2)
    keeping = jnp.where(which_half == 0, pieces[:, :, 0], pieces[:, :, 1])
    giving = jnp.where(which_half == 0, pieces[:, :, 1], pieces[:, :, 0])
    received = from_partner(giving, "tp", half_width.bit_length() - 1)
    return jnp.where(
        which_half == 0,
        jnp.concatenate([keeping, received], axis=0),
        jnp.concatenate([received, keeping], axis=0),
    )


def solution(mesh):
    placed = (P("dp", "tp", None), P("dp"), P(), P("dp", "tp"), P("dp", "tp"))
    return jax.shard_map(
        per_device, mesh=mesh, in_specs=placed, out_specs=P("dp", None, "tp"), check_vma=False
    )
```

profile of v0, /device:TPU:32, one launch (start us, length us, event | category | flops | bytes accessed | tf_op | source)
XLA Modules:
  0.0 855.2 jit_solution(84260706892302225)
XLA Ops:
  7.4 0.7 all-gather.9.cloned.1.call-update
  8.1 231.1 %all-gather.9.cloned.1.call-done = bf16[32,288,64]{1,2,0:T(8,128)(2,1)} async-done(((bf16[1,288,64]{1,2,0:T(8,128)(2,1)}), bf16[32,288,64]{1,2,0:T(8,128)(2,1)}) %all-gather.9.cloned.1.call-update) | async-done | bytes 1179664 | tf_op jit(solution)/shard_map/all_gather | solution.py:102
  239.1 2.3 copy.30
  241.5 1.1 reshape.402
  242.5 1.4 copy.31
  243.9 7.0 all-to-all-start
  251.0 0.7 all-gather.7.cloned.1.call-update
  251.7 237.4 %all-gather.7.cloned.1.call-done = bf16[1024,512]{1,0:T(8,128)(2,1)} async-done(((bf16[32,512]{1,0:T(8,128)(2,1)}), bf16[1024,512]{1,0:T(8,128)(2,1)}) %all-gather.7.cloned.1.call-update) | async-done | bytes 1048592 | tf_op jit(solution)/shard_map/all_gather | solution.py:103
  489.1 8.2 all-to-all-start.2
  497.5 0.8 gather_fusion
  498.9 2.6 copy.32
  501.4 46.3 %all-to-all-done.2 = bf16[16,64,512]{2,1,0:T(8,128)(2,1)} async-done(((bf16[16,64,512]{2,1,0:T(8,128)(2,1)}), bf16[16,64,512]{2,1,0:T(8,128)(2,1)}, u32[]{:S(2)}, u32[]{:S(2)}) %all-to-all-start.2) | async-done | bytes 1048608 | tf_op jit(solution)/shard_map/all_to_all | solution.py:33
  547.8 3.8 all-to-all-start.1
  552.3 1.8 gather_fusion.1
  554.5 1.6 pad_maximum_fusion.1
  556.0 44.2 %all-to-all-done.1 = bf16[16,576,128]{2,1,0:T(8,128)(2,1)S(1)} async-done(((bf16[16,576,128]{2,1,0:T(8,128)(2,1)}), bf16[16,576,128]{2,1,0:T(8,128)(2,1)S(1)}, u32[]{:S(2)}, u32[]{:S(2)}) %all-to-all-start.1) | async-done | bytes 2359328 | tf_op jit(solution)/shard_map/all_to_all | solution.py:57
  600.2 44.0 %all-to-all-start.3 = ((bf16[16,64,1024]{2,1,0:T(8,128)(2,1)}), bf16[16,64,1024]{2,1,0:T(8,128)(2,1)}, u32[]{:S(2)}, u32[]{:S(2)}) async-start(bf16[16,64,1024]{2,1,0:T(8,128)(2,1)} %pad_maximum_fusion.1), calls=%async_computation.3 | async-start | bytes 4194304 | tf_op jit(solution)/shard_map/all_to_all | solution.py:58
  644.3 0.6 dynamic_slice.6
  646.8 150.8 %all-gather.5.cloned.1.call-done = bf16[2,576,1024]{2,0,1:T(2,128)(2,1)} async-done(((bf16[2,36,1024]{2,0,1:T(2,128)(2,1)}), bf16[2,576,1024]{2,0,1:T(2,128)(2,1)}) %all-gather.5.cloned.1.call-update) | async-done | bytes 2359312 | tf_op jit(solution)/shard_map/all_gather | solution.py:106
  797.6 4.1 constant_dynamic-slice_fusion
  804.2 0.6 fusion.39
  806.4 0.6 bitcast_add_fusion
  807.3 2.2 collective-permute-start
  809.5 0.9 collective-permute-done
  810.4 2.2 collective-permute-start.1
  812.6 4.1 collective-permute-done.1
  816.8 3.3 collective-permute-start.2
  820.2 5.2 collective-permute-done.2
  825.4 2.1 convolution_convert_fusion
  828.1 2.7 collective-permute-start.3
  830.8 16.2 %collective-permute-done.3 = bf16[1,144,512]{2,1,0:T(8,128)(2,1)S(1)} collective-permute-done((bf16[1,144,512]{2,1,0:T(8,128)(2,1)S(1)}, bf16[1,144,512]{2,1,0:T(8,128)(2,1)S(1)}, u32[]{:S(2)}, u32[]{:S(2)}) %collective-permute-start.3) | collective-permute-done | bytes 147488 | tf_op jit(solution)/shard_map/ppermute | solution.py:10
  847.1 0.7 maximum_select_fusion.2
  (40 shorter events, 6.9 us)
Async XLA Ops:
  7.4 231.8 %all-gather.9.cloned.1.call-start = ((), (), s32[]{:S(2)}) async-start(), calls=%async_computation.6 | async-start | bytes 1622016 | tf_op jit(solution)/shard_map/all_gather | solution.py:102
  243.9 245.2 %all-to-all-start = ((bf16[16,576,64]{1,2,0:T(8,128)(2,1)}), bf16[16,576,64]{1,2,0:T(8,128)(2,1)S(1)}, u32[]{:S(2)}, u32[]{:S(2)}) async-start(bf16[16,576,64]{1,2,0:T(8,128)(2,1)} %copy.31), calls=%async_computation | async-start | bytes 2621440 | tf_op jit(solution)/shard_map/all_to_all | solution.py:26
  250.9 246.4 %copy-start = (s32[16]{0:T(128)S(1)}, s32[16]{0:T(128)}, u32[]{:S(2)}) copy-start(s32[16]{0:T(128)} %param.7) | copy-start | bytes 196
  250.9 238.2 %all-gather.7.cloned.1.call-start = ((), (), s32[]{:S(2)}) async-start(), calls=%async_computation.5 | async-start | bytes 1081344 | tf_op jit(solution)/shard_map/all_gather | solution.py:103
  489.1 58.7 %all-to-all-start.2 = ((bf16[16,64,512]{2,1,0:T(8,128)(2,1)}), bf16[16,64,512]{2,1,0:T(8,128)(2,1)}, u32[]{:S(2)}, u32[]{:S(2)}) async-start(bf16[16,64,512]{2,1,0:T(8,128)(2,1)} %bitcast.127), calls=%async_computation.2 | async-start | bytes 2097152 | tf_op jit(solution)/shard_map/all_to_all | solution.py:33
  547.8 52.4 %all-to-all-start.1 = ((bf16[16,576,128]{2,1,0:T(8,128)(2,1)}), bf16[16,576,128]{2,1,0:T(8,128)(2,1)S(1)}, u32[]{:S(2)}, u32[]{:S(2)}) async-start(bf16[16,576,128]{2,1,0:T(8,128)(2,1)} %copy.32), calls=%async_computation.1 | async-start | bytes 4718592 | tf_op jit(solution)/shard_map/all_to_all | solution.py:57
  551.6 246.0 %all-gather.5.cloned.1.call-start = ((), (), s32[]{:S(2)}) async-start(), calls=%async_computation.4 | async-start | bytes 2506752 | tf_op jit(solution)/shard_map/all_gather | solution.py:106
  556.0 88.3 %copy-start.1 = (s32[2]{0:T(128)S(1)}, s32[2]{0:T(128)}, u32[]{:S(2)}) copy-start(s32[2]{0:T(128)} %param.6) | copy-start | bytes 28
  600.2 220.0 %all-to-all-start.3 = ((bf16[16,64,1024]{2,1,0:T(8,128)(2,1)}), bf16[16,64,1024]{2,1,0:T(8,128)(2,1)}, u32[]{:S(2)}, u32[]{:S(2)}) async-start(bf16[16,64,1024]{2,1,0:T(8,128)(2,1)} %pad_maximum_fusion.1), calls=%async_computation.3 | async-start | bytes 4194304 | tf_op jit(solution)/shard_map/all_to_all | solution.py:58
  807.3 3.1 collective-permute-start
  810.4 6.3 collective-permute-start.1
  816.8 8.6 %collective-permute-start.2 = (bf16[1,144,512]{2,1,0:T(8,128)(2,1)S(1)}, bf16[1,144,512]{2,1,0:T(8,128)(2,1)S(1)}, u32[]{:S(2)}, u32[]{:S(2)}) collective-permute-start(bf16[1,144,512]{2,1,0:T(8,128)(2,1)S(1)} %maximum_select_fusion.3), channel_id=1, source_target_pairs={{0,4},{1,5},{2,6},{3,7},{4,0},{5,1},{6,2},{7,3},{8,12},{9,13},{10,... | collective-permute-start | bytes 442376 | tf_op jit(solution)/shard_map/ppermute | solution.py:10
  828.1 18.9 %collective-permute-start.3 = (bf16[1,144,512]{2,1,0:T(8,128)(2,1)S(1)}, bf16[1,144,512]{2,1,0:T(8,128)(2,1)S(1)}, u32[]{:S(2)}, u32[]{:S(2)}) collective-permute-start(bf16[1,144,512]{2,1,0:T(8,128)(2,1)S(1)} %get-tuple-element.17), channel_id=1, source_target_pairs={{0,8},{1,9},{2,10},{3,11},{4,12},{5,13},{6,14},{7,15},{8,0},{9,1},... | collective-permute-start | bytes 442376 | tf_op jit(solution)/shard_map/ppermute | solution.py:10
Sparse Core Ops, SparseCore 0:
  10.3 228.8 all-gather.8
  253.8 235.2 all-gather.6
Sparse Core Ops, SparseCore 1:
  555.4 242.2 all-gather.4
where the time goes:
time: 856 us; the launch traced here: 855 us
  waiting for transfers between devices  738 us (86%)
  starting transfers between devices  73.4 us (9%)
  between operations  17.2 us (2%)
  local copies, waits for them, and re-layouts  15.6 us (2%)
    all_gather x1, waiting for transfers between devices, per_device(): lax.all_gather(proj_weight, 'dp', axis=0, tiled=True)  237 us
    all_gather x1, waiting for transfers between devices, per_device(): lax.all_gather(conv_weight, 'dp', axis=0, tiled=True)  231 us
    all_gather x1, waiting for transfers between devices, per_device(): gathered = lax.all_gather(patches, 'tp', axis=1, tiled=True)  151 us
    all_to_all x1, waiting for transfers between devices, relayout(): lax.all_to_all(proj_part.reshape(tp_count, proj_rows, proj_block), 'tp',...  46.3 us
    all_to_all x1, waiting for transfers between devices, relayout(): lax.all_to_all(send_conv, 'tp', split_axis=0, concat_axis=0, tiled=True)  44.2 us
    all_to_all x1, starting transfers between devices, relayout(): lax.all_to_all(send_proj, 'tp', split_axis=0, concat_axis=0, tiled=True)  44 us
    ppermute x4, waiting for transfers between devices, from_partner(): lax.ppermute(value, axis, [(i, i ^ 1 << apart) for i in range(lax.axis_si...  26.4 us
  transfers between devices with their start and end apart: 11, of which 9 were waited for; matrix products, arithmetic and copies ran while one was open for 2% of the time, Pallas kernels for 0%

commit v1 on v0

v1 whole, which is shorter than its diff:
```python
import functools

import jax
import jax.numpy as jnp
from jax import lax
from jax.experimental import pallas as pl
from jax.experimental.pallas import tpu as pltpu
from jax.sharding import PartitionSpec as P

MESH = pl.DeviceIdType.MESH

GRID = 24
NX, NY, NZ = 4, 4, 8
SLOTS = 2 * NX
SLOT_ROWS = 80
CHIP_ROWS = 72


class Place:
    def __init__(self):
        d = lax.axis_index("dp")
        t = lax.axis_index("tp")
        self.y, self.z = d // NZ, lax.rem(d, NZ)
        self.h, self.x, self.c = t // (2 * NX), lax.rem(t // 2, NX), lax.rem(t, 2)
        self.d, self.t = d, t
        self.slot = self.h * NX + self.x

    def at(self, y=None, z=None, h=None, x=None, c=None):
        y = self.y if y is None else y
        z = self.z if z is None else z
        h = self.h if h is None else h
        x = self.x if x is None else x
        c = self.c if c is None else c
        return (y * NZ + z, h * (2 * NX) + x * 2 + c)

    def sibling(self):
        return self.at(c=1 - self.c)

    def flip(self):
        return self.at(h=1 - self.h)


def plus(value, step, size):
    return lax.rem(value + step, size)


def kernel(
    tb_ref,
    slot_ref,
    patches,
    conv,
    proj,
    out_ref,
    tokens,
    halves,
    grid_img,
    weights,
    z_ref,
    fs_ref,
    pooled,
    proj_all,
    proj_cols,
    proj_perm,
    loc,
    ce_s,
    ce_r,
    wz_s,
    wz_r,
    wy_s,
    wy_r,
    wd_s,
    wd_r,
    gz_s,
    gz_r,
    gx_s,
    gx_r,
    pz_s,
    pz_r,
    px_s,
    px_r,
    pd_s,
    pd_r,
    qz_s,
    qz_r,
    qy_s,
    qy_r,
    oz_s,
    oz_r,
    ox_s,
    ox_r,
    od_s,
    od_r,
):
    me = Place()
    c, h, x, y, z, d = me.c, me.h, me.x, me.y, me.z, me.d
    other = 1 - c
    sibling, flip = me.sibling(), me.flip()
    my_slot = me.slot
    flip_slot = (1 - h) * NX + x

    def remote(src, dst, send, recv, where):
        return pltpu.make_async_remote_copy(
            src_ref=src, dst_ref=dst, send_sem=send, recv_sem=recv, device_id=where, device_id_type=MESH
        )

    def await_recv(dst, recv):
        remote(dst, dst, recv, recv, sibling).wait_recv()

    def await_send(src, send):
        remote(src, src, send, send, sibling).wait_send()

    barrier = pltpu.get_barrier_semaphore()

    def greet(where):
        pl.semaphore_signal(barrier, inc=1, device_id=where, device_id_type=MESH)

    greet(flip)
    for k in range(1, NZ):
        greet(me.at(z=plus(z, k, NZ)))
    for k in range(1, NX):
        greet(me.at(x=plus(x, k, NX)))
    for k in range(1, NY):
        greet(me.at(y=plus(y, k, NY)))
    greet(sibling)

    own_rows = pl.ds(pl.multiple_of(c * 144, 16), 144)
    other_rows = pl.ds(pl.multiple_of(other * 144, 16), 144)
    local = [
        pltpu.make_async_copy(patches.at[c], tokens.at[c], loc.at[0]),
        pltpu.make_async_copy(conv.at[own_rows], halves.at[c], loc.at[1]),
        pltpu.make_async_copy(proj, proj_all.at[c, my_slot], loc.at[2]),
    ]
    for copy in local:
        copy.start()

    row = lax.broadcasted_iota(jnp.int32, (1024, 128), 0)
    lane = lax.broadcasted_iota(jnp.int32, (1024, 128), 1)
    first = tb_ref[2 * my_slot] * 64
    second = tb_ref[2 * my_slot + 1] * 64 - 64
    wanted = lane + jnp.where(lane < 64, first, second)
    weights[pl.ds(9 * 1024, 1024), :] = jnp.where(row == wanted, 1.0, 0.0).astype(jnp.bfloat16)

    for copy in local:
        copy.wait()
    pl.semaphore_wait(barrier, 1 + (NZ - 1) + (NX - 1) + (NY - 1) + 1)

    ce_conv = remote(conv.at[other_rows], halves.at[c], ce_s.at[0], ce_r.at[0], sibling)
    ce_conv.start()
    ce_img = remote(patches.at[other], tokens.at[c], ce_s.at[1], ce_r.at[1], sibling)
    ce_img.start()
    own_proj = proj_all.at[c, my_slot]
    remote(own_proj, own_proj, pz_s, pz_r, flip).start()
    for k in range(1, NX):
        remote(own_proj, own_proj, px_s.at[k - 1], px_r.at[k - 1], me.at(x=plus(x, k, NX))).start()

    def shard(dp, core):
        return weights.at[pl.ds(pl.multiple_of(dp * 288 + core * 144, 16), 144)]

    await_recv(halves.at[other], ce_r.at[0])
    own_shard = shard(d, c)
    own_shard[...] = jnp.concatenate([halves[0], halves[1]], axis=1)
    for k in range(1, NZ):
        remote(own_shard, own_shard, wz_s.at[k - 1], wz_r.at[k - 1], me.at(z=plus(z, k, NZ))).start()

    await_recv(tokens.at[other], ce_r.at[1])
    chip_tokens = jnp.concatenate(
        [tokens[0].astype(jnp.float32), tokens[1].astype(jnp.float32), jnp.zeros((SLOT_ROWS - CHIP_ROWS, 1024), jnp.float32)],
        axis=0,
    )

    def image(slot):
        return grid_img.at[pl.ds(pl.multiple_of(slot * SLOT_ROWS, 16), SLOT_ROWS)]

    own_img = image(my_slot)
    own_img[...] = chip_tokens.astype(jnp.bfloat16)
    remote(own_img, own_img, gz_s, gz_r, flip).start()
    for k in range(1, NX):
        remote(own_img, own_img, gx_s.at[k - 1], gx_r.at[k - 1], me.at(x=plus(x, k, NX))).start()

    def shard_to_y(k):
        piece = shard(y * NZ + lax.rem(z - k + NZ, NZ), c)
        for j in range(1, NY):
            remote(
                piece, piece, wy_s.at[(j - 1) * NZ + k], wy_r.at[(j - 1) * NZ + k], me.at(y=plus(y, j, NY))
            ).start()

    shard_to_y(0)

    @pl.loop(1, NZ)
    def _(k):
        await_recv(shard(y * NZ + lax.rem(z - k + NZ, NZ), c), wz_r.at[k - 1])
        shard_to_y(k)

    def to_sibling(dp, index):
        piece = shard(dp, c)
        remote(piece, piece, wd_s.at[index], wd_r.at[index], sibling).start()

    @pl.loop(0, NZ)
    def _(k):
        to_sibling(y * NZ + lax.rem(z - k + NZ, NZ), k)

    flip_proj = proj_all.at[c, flip_slot]
    await_recv(flip_proj, pz_r)
    for k in range(1, NX):
        remote(flip_proj, flip_proj, px_s.at[2 + k], px_r.at[2 + k], me.at(x=plus(x, k, NX))).start()

    flip_img = image(flip_slot)
    await_recv(flip_img, gz_r)
    for k in range(1, NX):
        remote(flip_img, flip_img, gx_s.at[2 + k], gx_r.at[2 + k], me.at(x=plus(x, k, NX))).start()

    for k in range(1, NX):
        src_x = plus(x, NX - k, NX)
        await_recv(proj_all.at[c, h * NX + src_x], px_r.at[k - 1])
        await_recv(proj_all.at[c, (1 - h) * NX + src_x], px_r.at[2 + k])
    remote(proj_all.at[c], proj_all.at[c], pd_s, pd_r, sibling).start()
    await_recv(proj_all.at[other], pd_r)
    holder = jnp.int32(0)
    for t in range(4 * NX):
        holder = jnp.where(tb_ref[t] == me.t, t, holder)
    own_cols = proj_cols.at[d]
    own_cols[...] = proj_all[lax.rem(holder, 2), holder // 2]
    for k in range(1, NZ):
        remote(own_cols, own_cols, qz_s.at[k - 1], qz_r.at[k - 1], me.at(z=plus(z, k, NZ))).start()

    for j in range(1, NY):
        src_y = plus(y, NY - j, NY)

        @pl.loop(0, NZ)
        def _(k, j=j, src_y=src_y):
            src_d = src_y * NZ + lax.rem(z - k + NZ, NZ)
            await_recv(shard(src_d, c), wy_r.at[(j - 1) * NZ + k])
            to_sibling(src_d, j * NZ + k)

    for k in range(1, NX):
        src_x = plus(x, NX - k, NX)
        await_recv(image(h * NX + src_x), gx_r.at[k - 1])
        await_recv(image((1 - h) * NX + src_x), gx_r.at[2 + k])

    for j in range(NY):
        src_y = plus(y, NY - j, NY)

        @pl.loop(0, NZ)
        def _(k, j=j, src_y=src_y):
            src_d = src_y * NZ + lax.rem(z - k + NZ, NZ)
            await_recv(shard(src_d, other), wd_r.at[j * NZ + k])

    @pl.loop(0, 5)
    def _(n):
        rhs = jnp.concatenate(
            [
                weights[pl.ds(pl.multiple_of(n * 2048, 1024), 1024), :],
                weights[pl.ds(pl.multiple_of(n * 2048 + 1024, 1024), 1024), :],
            ],
            axis=1,
        )
        prod = jnp.dot(grid_img[...], rhs, preferred_element_type=jnp.float32)
        z_ref[2 * n] = prod[:, :128]
        z_ref[2 * n + 1] = prod[:, 128:]

    column = lax.broadcasted_iota(jnp.int32, (GRID, 128), 0)

    def product(tap, gy):
        return z_ref[tap, pl.ds((gy // 3) * SLOT_ROWS + (gy % 3) * GRID, GRID), :]

    for gy in range(0, GRID, 2):
        total = jnp.zeros((GRID, 128), jnp.float32)
        for row_y in (gy, gy + 1):
            parts = []
            for kx in range(3):
                part = None
                for ky in range(3):
                    if 0 <= row_y + ky - 1 < GRID:
                        value = product(3 * ky + kx, row_y + ky - 1)
                        part = value if part is None else part + value
                parts.append(part)
            left = jnp.where(column == 0, 0.0, pltpu.roll(parts[0], 1, 0))
            right = jnp.where(column == GRID - 1, 0.0, pltpu.roll(parts[2], GRID - 1, 0))
            value = parts[1] + left + right
            total = total + product(9, row_y) + value / (1.0 + jnp.exp(-value))
        fs_ref[pl.ds((gy // 2) * GRID, GRID), :] = total
    mean = (fs_ref[pl.ds(0, 144, stride=2), :] + fs_ref[pl.ds(1, 144, stride=2), :]) * 0.25
    own_pool = pooled.at[c, my_slot]
    own_pool[...] = mean.astype(jnp.bfloat16)

    remote(own_pool, own_pool, oz_s, oz_r, flip).start()
    for k in range(1, NX):
        remote(own_pool, own_pool, ox_s.at[k - 1], ox_r.at[k - 1], me.at(x=plus(x, k, NX))).start()

    def cols_to_y(k):
        piece = proj_cols.at[y * NZ + lax.rem(z - k + NZ, NZ)]
        for j in range(1, NY):
            remote(
                piece, piece, qy_s.at[(j - 1) * NZ + k], qy_r.at[(j - 1) * NZ + k], me.at(y=plus(y, j, NY))
            ).start()

    cols_to_y(0)

    @pl.loop(1, NZ)
    def _(k):
        await_recv(proj_cols.at[y * NZ + lax.rem(z - k + NZ, NZ)], qz_r.at[k - 1])
        cols_to_y(k)

    flip_pool = pooled.at[c, flip_slot]
    await_recv(flip_pool, oz_r)
    for k in range(1, NX):
        remote(flip_pool, flip_pool, ox_s.at[2 + k], ox_r.at[2 + k], me.at(x=plus(x, k, NX))).start()

    for j in range(1, NY):
        src_y = plus(y, NY - j, NY)

        @pl.loop(0, NZ)
        def _(k, j=j, src_y=src_y):
            src_d = src_y * NZ + lax.rem(z - k + NZ, NZ)
            await_recv(proj_cols.at[src_d], qy_r.at[(j - 1) * NZ + k])

    for t in range(4 * NX):
        block = tb_ref[t]
        proj_perm[pl.ds(t * 64, 32), :] = proj_cols[2 * block]
        proj_perm[pl.ds(t * 64 + 32, 32), :] = proj_cols[2 * block + 1]

    for k in range(1, NX):
        src_x = plus(x, NX - k, NX)
        await_recv(pooled.at[c, h * NX + src_x], ox_r.at[k - 1])
        await_recv(pooled.at[c, (1 - h) * NX + src_x], ox_r.at[2 + k])
    remote(pooled.at[c], pooled.at[c], od_s, od_r, sibling).start()
    await_recv(pooled.at[other], od_r)

    for slot in range(2):
        index = slot_ref[slot]
        lhs = jnp.concatenate([pooled[index, s] for s in range(SLOTS)], axis=1)
        out_ref[slot] = jnp.dot(lhs, proj_perm[...], preferred_element_type=jnp.float32).astype(jnp.bfloat16)

    ce_conv.wait_send()
    ce_img.wait_send()
    await_send(own_proj, pz_s)
    await_send(own_img, gz_s)
    await_send(own_pool, oz_s)
    await_send(proj_all.at[c], pd_s)
    await_send(pooled.at[c], od_s)
    for k in range(2 * (NX - 1)):
        await_send(own_proj, px_s.at[k])
        await_send(own_img, gx_s.at[k])
        await_send(own_pool, ox_s.at[k])

    @pl.loop(0, NZ - 1)
    def _(k):
        await_send(own_shard, wz_s.at[k])
        await_send(own_cols, qz_s.at[k])

    @pl.loop(0, (NY - 1) * NZ)
    def _(k):
        await_send(own_shard, wy_s.at[k])
        await_send(own_cols, qy_s.at[k])

    @pl.loop(0, NY * NZ)
    def _(k):
        await_send(own_shard, wd_s.at[k])


def per_device(patches, image_slot, trainer_blocks, conv_weight, proj_weight):
    dma = pltpu.SemaphoreType.DMA
    smem = pl.BlockSpec(memory_space=pltpu.SMEM)
    anywhere = pl.BlockSpec(memory_space=pl.ANY)
    bf16, f32 = jnp.bfloat16, jnp.float32
    pairs = [
        dma((2,)),
        dma((NZ - 1,)),
        dma(((NY - 1) * NZ,)),
        dma((NY * NZ,)),
        dma,
        dma((2 * (NX - 1),)),
        dma,
        dma((2 * (NX - 1),)),
        dma,
        dma((NZ - 1,)),
        dma(((NY - 1) * NZ,)),
        dma,
        dma((2 * (NX - 1),)),
        dma,
    ]
    return pl.pallas_call(
        kernel,
        out_shape=jax.ShapeDtypeStruct((2, 144, 512), bf16),
        in_specs=[smem, smem, anywhere, anywhere, anywhere],
        out_specs=pl.BlockSpec(memory_space=pltpu.VMEM),
        scratch_shapes=[
            pltpu.VMEM((2, 36, 1024), bf16),
            pltpu.VMEM((2, 144, 64), bf16),
            pltpu.VMEM((SLOTS * SLOT_ROWS, 1024), bf16),
            pltpu.VMEM((10 * 1024, 128), bf16),
            pltpu.VMEM((10, SLOTS * SLOT_ROWS, 128), f32),
            pltpu.VMEM((288, 128), f32),
            pltpu.VMEM((2, SLOTS, 144, 128), bf16),
            pltpu.VMEM((2, SLOTS, 32, 512), bf16),
            pltpu.VMEM((NY * NZ, 32, 512), bf16),
            pltpu.VMEM((1024, 512), bf16),
            dma((3,)),
        ]
        + [sem for sem in pairs for _ in range(2)],
        compiler_params=pltpu.CompilerParams(
            collective_id=0, has_side_effects=True, vmem_limit_bytes=40 * 1024 * 1024
        ),
        cost_estimate=pl.CostEstimate(flops=2_000_000_000, bytes_accessed=600_000, transcendentals=73728),
        name="vision",
    )(trainer_blocks, image_slot, patches, conv_weight, proj_weight)


def solution(mesh):
    placed = (P("dp", "tp", None), P("dp"), P(), P("dp", "tp"), P("dp", "tp"))
    return jax.shard_map(
        per_device, mesh=mesh, in_specs=placed, out_specs=P("dp", None, "tp"), check_vma=False
    )
```

time: 856 us -> 86.8 us (0.10)
  the two profiles are of different devices: /device:TPU:32 before, /device:TPU:65 now
where the time goes in v1:
time: 86.8 us; the launch traced here: 86.6 us
  Pallas kernels  84 us (97%)
  local copies, waits for them, and re-layouts  2.6 us (3%)
    pallas_call x1, Pallas kernels, per_device(): pl.pallas_call(kernel, out_shape=jax.ShapeDtypeStruct((2, 144, 512), bf16...  84 us
    unnamed x9, local copies, waits for them, and re-layouts  2.6 us

profile of v1, /device:TPU:65, one launch (start us, length us, event | category | flops | bytes accessed | tf_op | source)
XLA Modules:
  0.0 86.6 jit_solution(16596620854124528344)
XLA Ops:
  0.0 0.9 %copy.7.conv = bf16[288,64]{1,0:T(8,128)(2,1)S(1)} copy(bf16[288,64]{0,1:T(8,128)(2,1)} %param.8) | data formatting | bytes 73728 | tf_op args[3]
  0.9 0.0 copy-start
  0.9 0.0 copy-start.1
  0.9 0.0 copy-start.2
  1.0 1.0 %copy.6.patches = bf16[2,36,1024]{2,1,0:T(8,128)(2,1)S(1)} copy(bf16[2,36,1024]{2,0,1:T(2,128)(2,1)} %param.5) | data formatting | bytes 294912 | tf_op args[0]
  1.9 0.0 copy-done
  1.9 0.0 copy-done.1
  1.9 0.0 copy-done.2
  1.9 84.0 %vision.1 = bf16[2,144,512]{2,1,0:T(8,128)(2,1)S(1)} custom-call(s32[16]{0:T(128)S(1)} %copy-done.1, s32[2]{0:T(128)S(1)} %copy-done.2, bf16[2,36,1024]{2,1,0:T(8,128)(2,1)S(1)} %copy.6.patches, bf16[288,64]{1,0:T(8,128)(2,1)S(1)} %copy.7.conv, bf16[32,512]{1,0:T(8,128)(2,1)S(1)} %copy-done), custom_call_target="tpu_custom_call" | custom-call | flops 2000000000 | bytes 600000 | tf_op jit(solution)/shard_map/vision/pallas_call | solution.py:382
  85.9 0.7 copy.9
Async XLA Ops:
  0.9 1.0 %copy-start = (bf16[32,512]{1,0:T(8,128)(2,1)S(1)}, bf16[32,512]{1,0:T(8,128)(2,1)}, u32[]{:S(2)}) copy-start(bf16[32,512]{1,0:T(8,128)(2,1)} %proj.1) | copy-start | bytes 98308
  0.9 1.0 %copy-start.1 = (s32[16]{0:T(128)S(1)}, s32[16]{0:T(128)}, u32[]{:S(2)}) copy-start(s32[16]{0:T(128)} %tb_ref.1) | copy-start | bytes 196
  0.9 1.0 %copy-start.2 = (s32[2]{0:T(128)S(1)}, s32[2]{0:T(128)}, u32[]{:S(2)}) copy-start(s32[2]{0:T(128)} %slot_ref.1) | copy-start | bytes 28

commit v2 on v1

--- a/solution.py
+++ b/solution.py
@@ -14,6 +14,7 @@
 SLOTS = 2 * NX
 SLOT_ROWS = 80
 CHIP_ROWS = 72
+CUTS = ((0, 48), (48, 32))
 
 
 class Place:
@@ -61,6 +62,7 @@
     proj_all,
     proj_cols,
     proj_perm,
+    result,
     loc,
     ce_s,
     ce_r,
@@ -109,6 +111,11 @@
     def await_send(src, send):
         remote(src, src, send, send, sibling).wait_send()
 
+    bits = (lax.rem(z, 2), lax.rem(z // 2, 2), z // 4)
+
+    def across(m):
+        return sum((1 - bit if m >> i & 1 else bit) * (1 << i) for i, bit in enumerate(bits))
+
     barrier = pltpu.get_barrier_semaphore()
 
     def greet(where):
@@ -149,18 +156,54 @@
     ce_img = remote(patches.at[other], tokens.at[c], ce_s.at[1], ce_r.at[1], sibling)
     ce_img.start()
     own_proj = proj_all.at[c, my_slot]
+    flip_proj = proj_all.at[c, flip_slot]
     remote(own_proj, own_proj, pz_s, pz_r, flip).start()
-    for k in range(1, NX):
-        remote(own_proj, own_proj, px_s.at[k - 1], px_r.at[k - 1], me.at(x=plus(x, k, NX))).start()
+
+    def to_x(piece, sends, recvs, first):
+        for k in range(1, NX):
+            remote(piece, piece, sends.at[first + k - 1], recvs.at[first + k - 1], me.at(x=plus(x, k, NX))).start()
+
+    to_x(own_proj, px_s, px_r, 0)
 
     def shard(dp, core):
         return weights.at[pl.ds(pl.multiple_of(dp * 288 + core * 144, 16), 144)]
 
+    def w_piece(m, j=0):
+        return shard(plus(y, NY - j, NY) * NZ + across(m), c)
+
+    def q_piece(m, j=0):
+        return proj_cols.at[plus(y, NY - j, NY) * NZ + across(m)]
+
+    def to_z(piece, m, sends, recvs, partners):
+        for p in partners:
+            remote(piece(m), piece(m), sends.at[(m ^ p) - 1], recvs.at[(m ^ p) - 1], me.at(z=across(p))).start()
+
+    def to_y(piece, m, sends, recvs):
+        for j in range(1, NY):
+            i = (j - 1) * NZ + m
+            remote(piece(m), piece(m), sends.at[i], recvs.at[i], me.at(y=plus(y, j, NY))).start()
+
+    def w_sibling(m, j=0):
+        piece = w_piece(m, j)
+        remote(piece, piece, wd_s.at[j * NZ + m], wd_r.at[j * NZ + m], sibling).start()
+
+    def w_step(m, partners):
+        if m:
+            await_recv(w_piece(m), wz_r.at[m - 1])
+        to_z(w_piece, m, wz_s, wz_r, partners)
+        to_y(w_piece, m, wy_s, wy_r)
+        w_sibling(m)
+
+    def q_step(m, partners):
+        if m:
+            await_recv(q_piece(m), qz_r.at[m - 1])
+        to_z(q_piece, m, qz_s, qz_r, partners)
+        to_y(q_piece, m, qy_s, qy_r)
+
     await_recv(halves.at[other], ce_r.at[0])
-    own_shard = shard(d, c)
+    own_shard = w_piece(0)
     own_shard[...] = jnp.concatenate([halves[0], halves[1]], axis=1)
-    for k in range(1, NZ):
-        remote(own_shard, own_shard, wz_s.at[k - 1], wz_r.at[k - 1], me.at(z=plus(z, k, NZ))).start()
+    w_step(0, (4, 2, 1))
 
     await_recv(tokens.at[other], ce_r.at[1])
     chip_tokens = jnp.concatenate(
@@ -168,82 +211,65 @@
         axis=0,
     )
 
-    def image(slot):
-        return grid_img.at[pl.ds(pl.multiple_of(slot * SLOT_ROWS, 16), SLOT_ROWS)]
-
-    own_img = image(my_slot)
-    own_img[...] = chip_tokens.astype(jnp.bfloat16)
-    remote(own_img, own_img, gz_s, gz_r, flip).start()
-    for k in range(1, NX):
-        remote(own_img, own_img, gx_s.at[k - 1], gx_r.at[k - 1], me.at(x=plus(x, k, NX))).start()
-
-    def shard_to_y(k):
-        piece = shard(y * NZ + lax.rem(z - k + NZ, NZ), c)
-        for j in range(1, NY):
-            remote(
-                piece, piece, wy_s.at[(j - 1) * NZ + k], wy_r.at[(j - 1) * NZ + k], me.at(y=plus(y, j, NY))
-            ).start()
-
-    shard_to_y(0)
-
-    @pl.loop(1, NZ)
-    def _(k):
-        await_recv(shard(y * NZ + lax.rem(z - k + NZ, NZ), c), wz_r.at[k - 1])
-        shard_to_y(k)
-
-    def to_sibling(dp, index):
-        piece = shard(dp, c)
-        remote(piece, piece, wd_s.at[index], wd_r.at[index], sibling).start()
-
-    @pl.loop(0, NZ)
-    def _(k):
-        to_sibling(y * NZ + lax.rem(z - k + NZ, NZ), k)
-
-    flip_proj = proj_all.at[c, flip_slot]
+    def image(slot, first=0, count=SLOT_ROWS):
+        return grid_img.at[pl.ds(pl.multiple_of(slot * SLOT_ROWS + first, 16), count)]
+
+    image(my_slot)[...] = chip_tokens.astype(jnp.bfloat16)
+    for i, cut in enumerate(CUTS):
+        remote(image(my_slot, *cut), image(my_slot, *cut), gz_s.at[i], gz_r.at[i], flip).start()
+    to_x(image(my_slot), gx_s, gx_r, 0)
+
+    w_step(4, (2, 1))
+    w_step(2, (1,))
+    w_step(6, (1,))
+
     await_recv(flip_proj, pz_r)
-    for k in range(1, NX):
-        remote(flip_proj, flip_proj, px_s.at[2 + k], px_r.at[2 + k], me.at(x=plus(x, k, NX))).start()
-
-    flip_img = image(flip_slot)
-    await_recv(flip_img, gz_r)
-    for k in range(1, NX):
-        remote(flip_img, flip_img, gx_s.at[2 + k], gx_r.at[2 + k], me.at(x=plus(x, k, NX))).start()
+    to_x(flip_proj, px_s, px_r, NX - 1)
+
+    w_step(1, ())
+    w_step(5, ())
+    w_step(3, ())
+    w_step(7, ())
 
     for k in range(1, NX):
         src_x = plus(x, NX - k, NX)
         await_recv(proj_all.at[c, h * NX + src_x], px_r.at[k - 1])
-        await_recv(proj_all.at[c, (1 - h) * NX + src_x], px_r.at[2 + k])
+        await_recv(proj_all.at[c, (1 - h) * NX + src_x], px_r.at[NX - 1 + k - 1])
     remote(proj_all.at[c], proj_all.at[c], pd_s, pd_r, sibling).start()
     await_recv(proj_all.at[other], pd_r)
     holder = jnp.int32(0)
     for t in range(4 * NX):
         holder = jnp.where(tb_ref[t] == me.t, t, holder)
-    own_cols = proj_cols.at[d]
-    own_cols[...] = proj_all[lax.rem(holder, 2), holder // 2]
-    for k in range(1, NZ):
-        remote(own_cols, own_cols, qz_s.at[k - 1], qz_r.at[k - 1], me.at(z=plus(z, k, NZ))).start()
+    q_piece(0)[...] = proj_all[lax.rem(holder, 2), holder // 2]
+    q_step(0, (4, 2, 1))
+
+    def image_step(i):
+        await_recv(image(flip_slot, *CUTS[i]), gz_r.at[i])
+        to_x(image(flip_slot, *CUTS[i]), gx_s, gx_r, (1 + i) * (NX - 1))
+
+    image_step(0)
 
     for j in range(1, NY):
-        src_y = plus(y, NY - j, NY)
-
-        @pl.loop(0, NZ)
-        def _(k, j=j, src_y=src_y):
-            src_d = src_y * NZ + lax.rem(z - k + NZ, NZ)
-            await_recv(shard(src_d, c), wy_r.at[(j - 1) * NZ + k])
-            to_sibling(src_d, j * NZ + k)
+        for m in range(NZ):
+            await_recv(w_piece(m, j), wy_r.at[(j - 1) * NZ + m])
+            w_sibling(m, j)
+
+    image_step(1)
+
+    q_step(4, (2, 1))
+    q_step(2, (1,))
+    q_step(6, (1,))
+
+    for j in range(NY):
+        for m in range(NZ):
+            dp = plus(y, NY - j, NY) * NZ + across(m)
+            await_recv(shard(dp, other), wd_r.at[j * NZ + m])
 
     for k in range(1, NX):
         src_x = plus(x, NX - k, NX)
         await_recv(image(h * NX + src_x), gx_r.at[k - 1])
-        await_recv(image((1 - h) * NX + src_x), gx_r.at[2 + k])
-
-    for j in range(NY):
-        src_y = plus(y, NY - j, NY)
-
-        @pl.loop(0, NZ)
-        def _(k, j=j, src_y=src_y):
-            src_d = src_y * NZ + lax.rem(z - k + NZ, NZ)
-            await_recv(shard(src_d, other), wd_r.at[j * NZ + k])
+        for i, cut in enumerate(CUTS):
+            await_recv(image((1 - h) * NX + src_x, *cut), gx_r.at[(1 + i) * (NX - 1) + k - 1])
 
     @pl.loop(0, 5)
     def _(n):
@@ -284,35 +310,20 @@
     own_pool[...] = mean.astype(jnp.bfloat16)
 
     remote(own_pool, own_pool, oz_s, oz_r, flip).start()
-    for k in range(1, NX):
-        remote(own_pool, own_pool, ox_s.at[k - 1], ox_r.at[k - 1], me.at(x=plus(x, k, NX))).start()
-
-    def cols_to_y(k):
-        piece = proj_cols.at[y * NZ + lax.rem(z - k + NZ, NZ)]
-        for j in range(1, NY):
-            remote(
-                piece, piece, qy_s.at[(j - 1) * NZ + k], qy_r.at[(j - 1) * NZ + k], me.at(y=plus(y, j, NY))
-            ).start()
-
-    cols_to_y(0)
-
-    @pl.loop(1, NZ)
-    def _(k):
-        await_recv(proj_cols.at[y * NZ + lax.rem(z - k + NZ, NZ)], qz_r.at[k - 1])
-        cols_to_y(k)
+    to_x(own_pool, ox_s, ox_r, 0)
+
+    q_step(1, ())
+    q_step(5, ())
+    q_step(3, ())
+    q_step(7, ())
 
     flip_pool = pooled.at[c, flip_slot]
     await_recv(flip_pool, oz_r)
-    for k in range(1, NX):
-        remote(flip_pool, flip_pool, ox_s.at[2 + k], ox_r.at[2 + k], me.at(x=plus(x, k, NX))).start()
+    to_x(flip_pool, ox_s, ox_r, NX - 1)
 
     for j in range(1, NY):
-        src_y = plus(y, NY - j, NY)
-
-        @pl.loop(0, NZ)
-        def _(k, j=j, src_y=src_y):
-            src_d = src_y * NZ + lax.rem(z - k + NZ, NZ)
-            await_recv(proj_cols.at[src_d], qy_r.at[(j - 1) * NZ + k])
+        for m in range(NZ):
+            await_recv(q_piece(m, j), qy_r.at[(j - 1) * NZ + m])
 
     for t in range(4 * NX):
         block = tb_ref[t]
@@ -322,40 +333,50 @@
     for k in range(1, NX):
         src_x = plus(x, NX - k, NX)
         await_recv(pooled.at[c, h * NX + src_x], ox_r.at[k - 1])
-        await_recv(pooled.at[c, (1 - h) * NX + src_x], ox_r.at[2 + k])
+        await_recv(pooled.at[c, (1 - h) * NX + src_x], ox_r.at[NX - 1 + k - 1])
     remote(pooled.at[c], pooled.at[c], od_s, od_r, sibling).start()
     await_recv(pooled.at[other], od_r)
 
+    results = []
     for slot in range(2):
         index = slot_ref[slot]
         lhs = jnp.concatenate([pooled[index, s] for s in range(SLOTS)], axis=1)
-        out_ref[slot] = jnp.dot(lhs, proj_perm[...], preferred_element_type=jnp.float32).astype(jnp.bfloat16)
+        result[slot] = jnp.dot(lhs, proj_perm[...], preferred_element_type=jnp.float32).astype(jnp.bfloat16)
+        results.append(pltpu.make_async_copy(result.at[slot], out_ref.at[slot], loc.at[slot]))
+        results[-1].start()
 
     ce_conv.wait_send()
     ce_img.wait_send()
     await_send(own_proj, pz_s)
-    await_send(own_img, gz_s)
+    for i, cut in enumerate(CUTS):
+        await_send(image(my_slot, *cut), gz_s.at[i])
     await_send(own_pool, oz_s)
     await_send(proj_all.at[c], pd_s)
     await_send(pooled.at[c], od_s)
     for k in range(2 * (NX - 1)):
         await_send(own_proj, px_s.at[k])
-        await_send(own_img, gx_s.at[k])
         await_send(own_pool, ox_s.at[k])
+    for k in range(NX - 1):
+        await_send(image(my_slot), gx_s.at[k])
+        for i, cut in enumerate(CUTS):
+            await_send(image(my_slot, *cut), gx_s.at[(1 + i) * (NX - 1) + k])
 
     @pl.loop(0, NZ - 1)
     def _(k):
         await_send(own_shard, wz_s.at[k])
-        await_send(own_cols, qz_s.at[k])
+        await_send(q_piece(0), qz_s.at[k])
 
     @pl.loop(0, (NY - 1) * NZ)
     def _(k):
         await_send(own_shard, wy_s.at[k])
-        await_send(own_cols, qy_s.at[k])
+        await_send(q_piece(0), qy_s.at[k])
 
     @pl.loop(0, NY * NZ)
     def _(k):
         await_send(own_shard, wd_s.at[k])
+
+    for copy in results:
+        copy.wait()
 
 
 def per_device(patches, image_slot, trainer_blocks, conv_weight, proj_weight):
@@ -368,8 +389,8 @@
         dma((NZ - 1,)),
         dma(((NY - 1) * NZ,)),
         dma((NY * NZ,)),
-        dma,
-        dma((2 * (NX - 1),)),
+        dma((len(CUTS),)),
+        dma(((1 + len(CUTS)) * (NX - 1),)),
         dma,
         dma((2 * (NX - 1),)),
         dma,
@@ -383,7 +404,7 @@
         kernel,
         out_shape=jax.ShapeDtypeStruct((2, 144, 512), bf16),
         in_specs=[smem, smem, anywhere, anywhere, anywhere],
-        out_specs=pl.BlockSpec(memory_space=pltpu.VMEM),
+        out_specs=anywhere,
         scratch_shapes=[
             pltpu.VMEM((2, 36, 1024), bf16),
             pltpu.VMEM((2, 144, 64), bf16),
@@ -395,6 +416,7 @@
             pltpu.VMEM((2, SLOTS, 32, 512), bf16),
             pltpu.VMEM((NY * NZ, 32, 512), bf16),
             pltpu.VMEM((1024, 512), bf16),
+            pltpu.VMEM((2, 144, 512), bf16),
             dma((3,)),
         ]
         + [sem for sem in pairs for _ in range(2)],

time: 86.8 us -> 76.4 us (0.88)
  the two profiles are of different devices: /device:TPU:65 before, /device:TPU:1 now
where the time goes in v2:
time: 76.4 us; the launch traced here: 76.1 us
  Pallas kernels  73.4 us (96%)
  local copies, waits for them, and re-layouts  2.6 us (3%)
    pallas_call x1, Pallas kernels, per_device(): pl.pallas_call(kernel, out_shape=jax.ShapeDtypeStruct((2, 144, 512), bf16...  73.4 us
    unnamed x9, local copies, waits for them, and re-layouts  2.6 us

profile of v2, /device:TPU:1, one launch (start us, length us, event | category | flops | bytes accessed | tf_op | source)
XLA Modules:
  0.0 76.1 jit_solution(6359611643641696923)
XLA Ops:
  0.0 0.9 %copy.7.conv = bf16[288,64]{1,0:T(8,128)(2,1)S(1)} copy(bf16[288,64]{0,1:T(8,128)(2,1)} %param.8) | data formatting | bytes 73728 | tf_op args[3]
  0.9 0.0 copy-start
  0.9 0.0 copy-start.1
  0.9 0.0 copy-start.2
  1.0 1.0 %copy.6.patches = bf16[2,36,1024]{2,1,0:T(8,128)(2,1)S(1)} copy(bf16[2,36,1024]{2,0,1:T(2,128)(2,1)} %param.5) | data formatting | bytes 294912 | tf_op args[0]
  1.9 0.0 copy-done
  1.9 0.0 copy-done.1
  1.9 0.0 copy-done.2
  1.9 73.4 %vision.1 = bf16[2,144,512]{2,1,0:T(8,128)(2,1)S(1)} custom-call(s32[16]{0:T(128)S(1)} %copy-done.1, s32[2]{0:T(128)S(1)} %copy-done.2, bf16[2,36,1024]{2,1,0:T(8,128)(2,1)S(1)} %copy.6.patches, bf16[288,64]{1,0:T(8,128)(2,1)S(1)} %copy.7.conv, bf16[32,512]{1,0:T(8,128)(2,1)S(1)} %copy-done), custom_call_target="tpu_custom_call" | custom-call | flops 2000000000 | bytes 600000 | tf_op jit(solution)/shard_map/vision/pallas_call | solution.py:403
  75.3 0.7 copy.9
Async XLA Ops:
  0.9 1.0 %copy-start = (bf16[32,512]{1,0:T(8,128)(2,1)S(1)}, bf16[32,512]{1,0:T(8,128)(2,1)}, u32[]{:S(2)}) copy-start(bf16[32,512]{1,0:T(8,128)(2,1)} %proj.1) | copy-start | bytes 98308
  0.9 1.0 %copy-start.1 = (s32[16]{0:T(128)S(1)}, s32[16]{0:T(128)}, u32[]{:S(2)}) copy-start(s32[16]{0:T(128)} %tb_ref.1) | copy-start | bytes 196
  0.9 1.0 %copy-start.2 = (s32[2]{0:T(128)S(1)}, s32[2]{0:T(128)}, u32[]{:S(2)}) copy-start(s32[2]{0:T(128)} %slot_ref.1) | copy-start | bytes 28

commit v3 on v2

--- a/solution.py
+++ b/solution.py
@@ -65,32 +65,26 @@
     result,
     loc,
     ce_s,
+    w_s,
+    img_s,
+    proj_s,
+    proj_cs,
+    q_s,
+    pool_s,
+    pool_cs,
     ce_r,
-    wz_s,
     wz_r,
-    wy_s,
     wy_r,
-    wd_s,
     wd_r,
-    gz_s,
     gz_r,
-    gx_s,
     gx_r,
-    pz_s,
     pz_r,
-    px_s,
     px_r,
-    pd_s,
     pd_r,
-    qz_s,
     qz_r,
-    qy_s,
     qy_r,
-    oz_s,
     oz_r,
-    ox_s,
     ox_r,
-    od_s,
     od_r,
 ):
     me = Place()
@@ -157,13 +151,10 @@
     ce_img.start()
     own_proj = proj_all.at[c, my_slot]
     flip_proj = proj_all.at[c, flip_slot]
-    remote(own_proj, own_proj, pz_s, pz_r, flip).start()
-
-    def to_x(piece, sends, recvs, first):
+
+    def to_x(piece, send, recv):
         for k in range(1, NX):
-            remote(piece, piece, sends.at[first + k - 1], recvs.at[first + k - 1], me.at(x=plus(x, k, NX))).start()
-
-    to_x(own_proj, px_s, px_r, 0)
+            remote(piece, piece, send, recv, me.at(x=plus(x, k, NX))).start()
 
     def shard(dp, core):
         return weights.at[pl.ds(pl.multiple_of(dp * 288 + core * 144, 16), 144)]
@@ -174,36 +165,39 @@
     def q_piece(m, j=0):
         return proj_cols.at[plus(y, NY - j, NY) * NZ + across(m)]
 
-    def to_z(piece, m, sends, recvs, partners):
+    def to_z(piece, m, send, recvs, partners):
         for p in partners:
-            remote(piece(m), piece(m), sends.at[(m ^ p) - 1], recvs.at[(m ^ p) - 1], me.at(z=across(p))).start()
-
-    def to_y(piece, m, sends, recvs):
-        for j in range(1, NY):
-            i = (j - 1) * NZ + m
-            remote(piece(m), piece(m), sends.at[i], recvs.at[i], me.at(y=plus(y, j, NY))).start()
-
-    def w_sibling(m, j=0):
-        piece = w_piece(m, j)
-        remote(piece, piece, wd_s.at[j * NZ + m], wd_r.at[j * NZ + m], sibling).start()
+            remote(piece(m), piece(m), send, recvs.at[(m ^ p) - 1], me.at(z=across(p))).start()
+
+    def w_to_sibling(m, j):
+        remote(w_piece(m, j), w_piece(m, j), w_s, wd_r, sibling).start()
 
     def w_step(m, partners):
         if m:
             await_recv(w_piece(m), wz_r.at[m - 1])
-        to_z(w_piece, m, wz_s, wz_r, partners)
-        to_y(w_piece, m, wy_s, wy_r)
-        w_sibling(m)
+        to_z(w_piece, m, w_s, wz_r, partners)
+        for j in range(1, NY):
+            remote(w_piece(m), w_piece(m), w_s, wy_r.at[2 * (j - 1) + m % 2], me.at(y=plus(y, j, NY))).start()
+        w_to_sibling(m, 0)
+
+    def w_rest(j, odd):
+        await_recv(weights.at[pl.ds(0, 4 * 144)], wy_r.at[2 * (j - 1) + odd])
+        for m in range(odd, NZ, 2):
+            w_to_sibling(m, j)
 
     def q_step(m, partners):
         if m:
             await_recv(q_piece(m), qz_r.at[m - 1])
-        to_z(q_piece, m, qz_s, qz_r, partners)
-        to_y(q_piece, m, qy_s, qy_r)
+        to_z(q_piece, m, q_s, qz_r, partners)
+        for j in range(1, NY):
+            remote(q_piece(m), q_piece(m), q_s, qy_r, me.at(y=plus(y, j, NY))).start()
 
     await_recv(halves.at[other], ce_r.at[0])
     own_shard = w_piece(0)
     own_shard[...] = jnp.concatenate([halves[0], halves[1]], axis=1)
     w_step(0, (4, 2, 1))
+    remote(own_proj, own_proj, proj_s, pz_r, flip).start()
+    to_x(own_proj, proj_s, px_r)
 
     await_recv(tokens.at[other], ce_r.at[1])
     chip_tokens = jnp.concatenate(
@@ -215,27 +209,46 @@
         return grid_img.at[pl.ds(pl.multiple_of(slot * SLOT_ROWS + first, 16), count)]
 
     image(my_slot)[...] = chip_tokens.astype(jnp.bfloat16)
-    for i, cut in enumerate(CUTS):
-        remote(image(my_slot, *cut), image(my_slot, *cut), gz_s.at[i], gz_r.at[i], flip).start()
-    to_x(image(my_slot), gx_s, gx_r, 0)
-
+    to_x(image(my_slot), img_s, gx_r.at[0])
+
+    def flip_cut(i):
+        piece = image(my_slot, *CUTS[i])
+        remote(piece, piece, img_s, gz_r.at[i], flip).start()
+
+    def image_step(i):
+        piece = image(flip_slot, *CUTS[i])
+        await_recv(piece, gz_r.at[i])
+        to_x(piece, img_s, gx_r.at[1])
+
+    def multiply(half):
+        rows = pl.ds(pl.multiple_of(half * (NX * SLOT_ROWS), 64), NX * SLOT_ROWS)
+
+        @pl.loop(0, 5)
+        def _(n):
+            rhs = jnp.concatenate(
+                [
+                    weights[pl.ds(pl.multiple_of(n * 2048, 1024), 1024), :],
+                    weights[pl.ds(pl.multiple_of(n * 2048 + 1024, 1024), 1024), :],
+                ],
+                axis=1,
+            )
+            prod = jnp.dot(grid_img[rows, :], rhs, preferred_element_type=jnp.float32)
+            z_ref[2 * n, rows, :] = prod[:, :128]
+            z_ref[2 * n + 1, rows, :] = prod[:, 128:]
+
+    flip_cut(0)
     w_step(4, (2, 1))
+    flip_cut(1)
     w_step(2, (1,))
     w_step(6, (1,))
-
     await_recv(flip_proj, pz_r)
-    to_x(flip_proj, px_s, px_r, NX - 1)
-
+    to_x(flip_proj, proj_s, px_r)
     w_step(1, ())
     w_step(5, ())
+    await_recv(proj_all.at[c, pl.ds(0, 2 * (NX - 1))], px_r)
+    remote(proj_all.at[c], proj_all.at[c], proj_cs, pd_r, sibling).start()
     w_step(3, ())
     w_step(7, ())
-
-    for k in range(1, NX):
-        src_x = plus(x, NX - k, NX)
-        await_recv(proj_all.at[c, h * NX + src_x], px_r.at[k - 1])
-        await_recv(proj_all.at[c, (1 - h) * NX + src_x], px_r.at[NX - 1 + k - 1])
-    remote(proj_all.at[c], proj_all.at[c], pd_s, pd_r, sibling).start()
     await_recv(proj_all.at[other], pd_r)
     holder = jnp.int32(0)
     for t in range(4 * NX):
@@ -243,46 +256,20 @@
     q_piece(0)[...] = proj_all[lax.rem(holder, 2), holder // 2]
     q_step(0, (4, 2, 1))
 
-    def image_step(i):
-        await_recv(image(flip_slot, *CUTS[i]), gz_r.at[i])
-        to_x(image(flip_slot, *CUTS[i]), gx_s, gx_r, (1 + i) * (NX - 1))
-
     image_step(0)
-
     for j in range(1, NY):
-        for m in range(NZ):
-            await_recv(w_piece(m, j), wy_r.at[(j - 1) * NZ + m])
-            w_sibling(m, j)
-
+        w_rest(j, 0)
+    for j in range(1, NY):
+        w_rest(j, 1)
     image_step(1)
-
     q_step(4, (2, 1))
+    await_recv(weights.at[pl.ds(0, NY * NZ * 144)], wd_r)
+    await_recv(grid_img.at[pl.ds(0, (NX - 1) * SLOT_ROWS)], gx_r.at[0])
+    multiply(h)
     q_step(2, (1,))
     q_step(6, (1,))
-
-    for j in range(NY):
-        for m in range(NZ):
-            dp = plus(y, NY - j, NY) * NZ + across(m)
-            await_recv(shard(dp, other), wd_r.at[j * NZ + m])
-
-    for k in range(1, NX):
-        src_x = plus(x, NX - k, NX)
-        await_recv(image(h * NX + src_x), gx_r.at[k - 1])
-        for i, cut in enumerate(CUTS):
-            await_recv(image((1 - h) * NX + src_x, *cut), gx_r.at[(1 + i) * (NX - 1) + k - 1])
-
-    @pl.loop(0, 5)
-    def _(n):
-        rhs = jnp.concatenate(
-            [
-                weights[pl.ds(pl.multiple_of(n * 2048, 1024), 1024), :],
-                weights[pl.ds(pl.multiple_of(n * 2048 + 1024, 1024), 1024), :],
-            ],
-            axis=1,
-        )
-        prod = jnp.dot(grid_img[...], rhs, preferred_element_type=jnp.float32)
-        z_ref[2 * n] = prod[:, :128]
-        z_ref[2 * n + 1] = prod[:, 128:]
+    await_recv(grid_img.at[pl.ds(0, (NX - 1) * SLOT_ROWS)], gx_r.at[1])
+    multiply(1 - h)
 
     column = lax.broadcasted_iota(jnp.int32, (GRID, 128), 0)
 
@@ -309,32 +296,22 @@
     own_pool = pooled.at[c, my_slot]
     own_pool[...] = mean.astype(jnp.bfloat16)
 
-    remote(own_pool, own_pool, oz_s, oz_r, flip).start()
-    to_x(own_pool, ox_s, ox_r, 0)
-
-    q_step(1, ())
-    q_step(5, ())
-    q_step(3, ())
-    q_step(7, ())
-
+    remote(own_pool, own_pool, pool_s, oz_r, flip).start()
+    to_x(own_pool, pool_s, ox_r)
+    for m in (1, 5, 3, 7):
+        q_step(m, ())
     flip_pool = pooled.at[c, flip_slot]
     await_recv(flip_pool, oz_r)
-    to_x(flip_pool, ox_s, ox_r, NX - 1)
-
-    for j in range(1, NY):
-        for m in range(NZ):
-            await_recv(q_piece(m, j), qy_r.at[(j - 1) * NZ + m])
+    to_x(flip_pool, pool_s, ox_r)
+    await_recv(proj_cols.at[pl.ds(0, (NY - 1) * NZ)], qy_r)
 
     for t in range(4 * NX):
         block = tb_ref[t]
         proj_perm[pl.ds(t * 64, 32), :] = proj_cols[2 * block]
         proj_perm[pl.ds(t * 64 + 32, 32), :] = proj_cols[2 * block + 1]
 
-    for k in range(1, NX):
-        src_x = plus(x, NX - k, NX)
-        await_recv(pooled.at[c, h * NX + src_x], ox_r.at[k - 1])
-        await_recv(pooled.at[c, (1 - h) * NX + src_x], ox_r.at[NX - 1 + k - 1])
-    remote(pooled.at[c], pooled.at[c], od_s, od_r, sibling).start()
+    await_recv(pooled.at[c, pl.ds(0, 2 * (NX - 1))], ox_r)
+    remote(pooled.at[c], pooled.at[c], pool_cs, od_r, sibling).start()
     await_recv(pooled.at[other], od_r)
 
     results = []
@@ -347,34 +324,13 @@
 
     ce_conv.wait_send()
     ce_img.wait_send()
-    await_send(own_proj, pz_s)
-    for i, cut in enumerate(CUTS):
-        await_send(image(my_slot, *cut), gz_s.at[i])
-    await_send(own_pool, oz_s)
-    await_send(proj_all.at[c], pd_s)
-    await_send(pooled.at[c], od_s)
-    for k in range(2 * (NX - 1)):
-        await_send(own_proj, px_s.at[k])
-        await_send(own_pool, ox_s.at[k])
-    for k in range(NX - 1):
-        await_send(image(my_slot), gx_s.at[k])
-        for i, cut in enumerate(CUTS):
-            await_send(image(my_slot, *cut), gx_s.at[(1 + i) * (NX - 1) + k])
-
-    @pl.loop(0, NZ - 1)
-    def _(k):
-        await_send(own_shard, wz_s.at[k])
-        await_send(q_piece(0), qz_s.at[k])
-
-    @pl.loop(0, (NY - 1) * NZ)
-    def _(k):
-        await_send(own_shard, wy_s.at[k])
-        await_send(q_piece(0), qy_s.at[k])
-
-    @pl.loop(0, NY * NZ)
-    def _(k):
-        await_send(own_shard, wd_s.at[k])
-
+    await_send(weights.at[pl.ds(0, (NZ - 1 + (NY - 1) * NZ + NY * NZ) * 144)], w_s)
+    await_send(grid_img.at[pl.ds(0, (2 * (NX - 1) + 1) * SLOT_ROWS)], img_s)
+    await_send(proj_all.at[c, pl.ds(0, 2 * (NX - 1) + 1)], proj_s)
+    await_send(proj_all.at[c], proj_cs)
+    await_send(proj_cols.at[pl.ds(0, NZ - 1 + (NY - 1) * NZ)], q_s)
+    await_send(pooled.at[c, pl.ds(0, 2 * (NX - 1) + 1)], pool_s)
+    await_send(pooled.at[c], pool_cs)
     for copy in results:
         copy.wait()
 
@@ -384,20 +340,28 @@
     smem = pl.BlockSpec(memory_space=pltpu.SMEM)
     anywhere = pl.BlockSpec(memory_space=pl.ANY)
     bf16, f32 = jnp.bfloat16, jnp.float32
-    pairs = [
+    sems = [
+        dma((2,)),
+        dma,
+        dma,
+        dma,
+        dma,
+        dma,
+        dma,
+        dma,
         dma((2,)),
         dma((NZ - 1,)),
-        dma(((NY - 1) * NZ,)),
-        dma((NY * NZ,)),
+        dma((2 * (NY - 1),)),
+        dma,
         dma((len(CUTS),)),
-        dma(((1 + len(CUTS)) * (NX - 1),)),
-        dma,
-        dma((2 * (NX - 1),)),
+        dma((2,)),
+        dma,
+        dma,
         dma,
         dma((NZ - 1,)),
-        dma(((NY - 1) * NZ,)),
-        dma,
-        dma((2 * (NX - 1),)),
+        dma,
+        dma,
+        dma,
         dma,
     ]
     return pl.pallas_call(
@@ -419,7 +383,7 @@
             pltpu.VMEM((2, 144, 512), bf16),
             dma((3,)),
         ]
-        + [sem for sem in pairs for _ in range(2)],
+        + sems,
         compiler_params=pltpu.CompilerParams(
             collective_id=0, has_side_effects=True, vmem_limit_bytes=40 * 1024 * 1024
         ),

time: 76.4 us -> 71.1 us (0.931)
  Pallas kernels: 73.4 us -> 68.3 us
    pallas_call x1, Pallas kernels: 73.4 us -> 68.3 us  [per_device(): pl.pallas_call(kernel, out_shape=jax.ShapeDtypeStruct((2, 144, 512), bf16...]
where the time goes in v3:
time: 71.1 us; the launch traced here: 70.9 us
  Pallas kernels  68.3 us (96%)
  local copies, waits for them, and re-layouts  2.6 us (4%)
    pallas_call x1, Pallas kernels, per_device(): pl.pallas_call(kernel, out_shape=jax.ShapeDtypeStruct((2, 144, 512), bf16...  68.3 us
    unnamed x9, local copies, waits for them, and re-layouts  2.6 us

profile of v3, /device:TPU:1, one launch (start us, length us, event | category | flops | bytes accessed | tf_op | source)
XLA Modules:
  0.0 70.9 jit_solution(7790912586026397782)
XLA Ops:
  0.0 0.9 %copy.7.conv = bf16[288,64]{1,0:T(8,128)(2,1)S(1)} copy(bf16[288,64]{0,1:T(8,128)(2,1)} %param.8) | data formatting | bytes 73728 | tf_op args[3]
  0.9 0.0 copy-start
  0.9 0.0 copy-start.1
  0.9 0.0 copy-start.2
  1.0 1.0 %copy.6.patches = bf16[2,36,1024]{2,1,0:T(8,128)(2,1)S(1)} copy(bf16[2,36,1024]{2,0,1:T(2,128)(2,1)} %param.5) | data formatting | bytes 294912 | tf_op args[0]
  1.9 0.0 copy-done
  1.9 0.0 copy-done.1
  1.9 0.0 copy-done.2
  1.9 68.3 %vision.1 = bf16[2,144,512]{2,1,0:T(8,128)(2,1)S(1)} custom-call(s32[16]{0:T(128)S(1)} %copy-done.1, s32[2]{0:T(128)S(1)} %copy-done.2, bf16[2,36,1024]{2,1,0:T(8,128)(2,1)S(1)} %copy.6.patches, bf16[288,64]{1,0:T(8,128)(2,1)S(1)} %copy.7.conv, bf16[32,512]{1,0:T(8,128)(2,1)S(1)} %copy-done), custom_call_target="tpu_custom_call" | custom-call | flops 2000000000 | bytes 600000 | tf_op jit(solution)/shard_map/vision/pallas_call | solution.py:367
  70.2 0.7 %copy.9 = bf16[2,144,512]{2,1,0:T(8,128)(2,1)} copy(bf16[2,144,512]{2,1,0:T(8,128)(2,1)S(1)} %vision.1) | data formatting | bytes 589824
Async XLA Ops:
  0.9 1.0 %copy-start = (bf16[32,512]{1,0:T(8,128)(2,1)S(1)}, bf16[32,512]{1,0:T(8,128)(2,1)}, u32[]{:S(2)}) copy-start(bf16[32,512]{1,0:T(8,128)(2,1)} %proj.1) | copy-start | bytes 98308
  0.9 1.0 %copy-start.1 = (s32[16]{0:T(128)S(1)}, s32[16]{0:T(128)}, u32[]{:S(2)}) copy-start(s32[16]{0:T(128)} %tb_ref.1) | copy-start | bytes 196
  0.9 1.0 %copy-start.2 = (s32[2]{0:T(128)S(1)}, s32[2]{0:T(128)}, u32[]{:S(2)}) copy-start(s32[2]{0:T(128)} %slot_ref.1) | copy-start | bytes 28

commit v4 on v3

--- a/solution.py
+++ b/solution.py
@@ -14,7 +14,8 @@
 SLOTS = 2 * NX
 SLOT_ROWS = 80
 CHIP_ROWS = 72
-CUTS = ((0, 48), (48, 32))
+BODY_ROWS = 64
+CUTS = ((0, 32), (32, 32))
 
 
 class Place:
@@ -46,15 +47,19 @@
 
 
 def kernel(
-    tb_ref,
-    slot_ref,
+    tb_in,
+    slot_in,
     patches,
     conv,
     proj,
     out_ref,
+    tb_ref,
+    slot_ref,
     tokens,
     halves,
+    pair_rows,
     grid_img,
+    rests,
     weights,
     z_ref,
     fs_ref,
@@ -62,11 +67,13 @@
     proj_all,
     proj_cols,
     proj_perm,
+    own_pool,
     result,
     loc,
     ce_s,
     w_s,
     img_s,
+    rest_s,
     proj_s,
     proj_cs,
     q_s,
@@ -78,6 +85,8 @@
     wd_r,
     gz_r,
     gx_r,
+    rz_r,
+    rx_r,
     pz_r,
     px_r,
     pd_r,
@@ -85,6 +94,7 @@
     qy_r,
     oz_r,
     ox_r,
+    oc_r,
     od_r,
 ):
     me = Place()
@@ -116,38 +126,33 @@
         pl.semaphore_signal(barrier, inc=1, device_id=where, device_id_type=MESH)
 
     greet(flip)
+    greet(me.at(h=1 - h, c=other))
     for k in range(1, NZ):
         greet(me.at(z=plus(z, k, NZ)))
     for k in range(1, NX):
         greet(me.at(x=plus(x, k, NX)))
+        greet(me.at(x=plus(x, k, NX), c=other))
     for k in range(1, NY):
         greet(me.at(y=plus(y, k, NY)))
     greet(sibling)
 
-    own_rows = pl.ds(pl.multiple_of(c * 144, 16), 144)
-    other_rows = pl.ds(pl.multiple_of(other * 144, 16), 144)
     local = [
-        pltpu.make_async_copy(patches.at[c], tokens.at[c], loc.at[0]),
-        pltpu.make_async_copy(conv.at[own_rows], halves.at[c], loc.at[1]),
+        pltpu.make_async_copy(patches, tokens.at[c], loc.at[0]),
+        pltpu.make_async_copy(conv, halves.at[c], loc.at[1]),
         pltpu.make_async_copy(proj, proj_all.at[c, my_slot], loc.at[2]),
+        pltpu.make_async_copy(tb_in, tb_ref, loc.at[3]),
+        pltpu.make_async_copy(slot_in, slot_ref, loc.at[4]),
     ]
     for copy in local:
         copy.start()
 
-    row = lax.broadcasted_iota(jnp.int32, (1024, 128), 0)
-    lane = lax.broadcasted_iota(jnp.int32, (1024, 128), 1)
-    first = tb_ref[2 * my_slot] * 64
-    second = tb_ref[2 * my_slot + 1] * 64 - 64
-    wanted = lane + jnp.where(lane < 64, first, second)
-    weights[pl.ds(9 * 1024, 1024), :] = jnp.where(row == wanted, 1.0, 0.0).astype(jnp.bfloat16)
-
     for copy in local:
         copy.wait()
-    pl.semaphore_wait(barrier, 1 + (NZ - 1) + (NX - 1) + (NY - 1) + 1)
-
-    ce_conv = remote(conv.at[other_rows], halves.at[c], ce_s.at[0], ce_r.at[0], sibling)
+    pl.semaphore_wait(barrier, 2 + (NZ - 1) + 2 * (NX - 1) + (NY - 1) + 1)
+
+    ce_conv = remote(halves.at[c], halves.at[c], ce_s.at[0], ce_r.at[0], sibling)
     ce_conv.start()
-    ce_img = remote(patches.at[other], tokens.at[c], ce_s.at[1], ce_r.at[1], sibling)
+    ce_img = remote(tokens.at[c], tokens.at[c], ce_s.at[1], ce_r.at[1], sibling)
     ce_img.start()
     own_proj = proj_all.at[c, my_slot]
     flip_proj = proj_all.at[c, flip_slot]
@@ -194,33 +199,58 @@
 
     await_recv(halves.at[other], ce_r.at[0])
     own_shard = w_piece(0)
-    own_shard[...] = jnp.concatenate([halves[0], halves[1]], axis=1)
+    both = jnp.concatenate([halves[0], halves[1]], axis=0).astype(jnp.float32)
+    both = jnp.concatenate([both, jnp.zeros((128, 96), jnp.float32)], axis=1)
+    pair_rows[...] = both.T[:288].astype(jnp.bfloat16)
+    own_shard[...] = pair_rows[pl.ds(pl.multiple_of(c * 144, 16), 144), :]
     w_step(0, (4, 2, 1))
     remote(own_proj, own_proj, proj_s, pz_r, flip).start()
     to_x(own_proj, proj_s, px_r)
 
     await_recv(tokens.at[other], ce_r.at[1])
-    chip_tokens = jnp.concatenate(
-        [tokens[0].astype(jnp.float32), tokens[1].astype(jnp.float32), jnp.zeros((SLOT_ROWS - CHIP_ROWS, 1024), jnp.float32)],
-        axis=0,
-    )
+    mine = [
+        jnp.where(c == 0, both[:, 0, :], both[:, 1, :]) for both in (tokens[i].astype(jnp.float32) for i in range(2))
+    ]
+    chip_tokens = jnp.concatenate(mine + [jnp.zeros((SLOT_ROWS - CHIP_ROWS, 1024), jnp.float32)], axis=0)
 
     def image(slot, first=0, count=SLOT_ROWS):
         return grid_img.at[pl.ds(pl.multiple_of(slot * SLOT_ROWS + first, 16), count)]
 
-    image(my_slot)[...] = chip_tokens.astype(jnp.bfloat16)
-    to_x(image(my_slot), img_s, gx_r.at[0])
+    image(my_slot, 0, BODY_ROWS)[...] = chip_tokens[:BODY_ROWS].astype(jnp.bfloat16)
+    own_rest = chip_tokens[BODY_ROWS:CHIP_ROWS]
+    rests[my_slot] = jnp.concatenate([own_rest[:, :512], own_rest[:, 512:]], axis=0).astype(jnp.bfloat16)
+    to_x(image(my_slot, 0, BODY_ROWS), img_s, gx_r.at[0])
+    to_x(rests.at[my_slot], rest_s, rx_r.at[0])
 
     def flip_cut(i):
         piece = image(my_slot, *CUTS[i])
         remote(piece, piece, img_s, gz_r.at[i], flip).start()
+
+    def flip_rest():
+        remote(rests.at[my_slot], rests.at[my_slot], rest_s, rz_r, flip).start()
 
     def image_step(i):
         piece = image(flip_slot, *CUTS[i])
         await_recv(piece, gz_r.at[i])
         to_x(piece, img_s, gx_r.at[1])
 
+    def rest_step():
+        await_recv(rests.at[flip_slot], rz_r)
+        to_x(rests.at[flip_slot], rest_s, rx_r.at[1])
+
+    def image_wait(which):
+        await_recv(grid_img.at[pl.ds(0, (NX - 1) * BODY_ROWS)], gx_r.at[which])
+        await_recv(rests.at[pl.ds(0, NX - 1)], rx_r.at[which])
+
+    def put_rests(half):
+        for i in range(NX):
+            rest = rests[half * NX + i].astype(jnp.float32)
+            rest = jnp.concatenate([rest[:8], rest[8:]], axis=1)
+            rest = jnp.concatenate([rest, jnp.zeros((8, 1024), jnp.float32)], axis=0)
+            image(half * NX + i, BODY_ROWS, 16)[...] = rest.astype(jnp.bfloat16)
+
     def multiply(half):
+        put_rests(half)
         rows = pl.ds(pl.multiple_of(half * (NX * SLOT_ROWS), 64), NX * SLOT_ROWS)
 
         @pl.loop(0, 5)
@@ -237,8 +267,15 @@
             z_ref[2 * n + 1, rows, :] = prod[:, 128:]
 
     flip_cut(0)
+    row = lax.broadcasted_iota(jnp.int32, (1024, 128), 0)
+    lane = lax.broadcasted_iota(jnp.int32, (1024, 128), 1)
+    first = tb_ref[2 * my_slot] * 64
+    second = tb_ref[2 * my_slot + 1] * 64 - 64
+    wanted = lane + jnp.where(lane < 64, first, second)
+    weights[pl.ds(9 * 1024, 1024), :] = jnp.where(row == wanted, 1.0, 0.0).astype(jnp.bfloat16)
     w_step(4, (2, 1))
     flip_cut(1)
+    flip_rest()
     w_step(2, (1,))
     w_step(6, (1,))
     await_recv(flip_proj, pz_r)
@@ -259,16 +296,17 @@
     image_step(0)
     for j in range(1, NY):
         w_rest(j, 0)
+    image_step(1)
+    rest_step()
     for j in range(1, NY):
         w_rest(j, 1)
-    image_step(1)
     q_step(4, (2, 1))
     await_recv(weights.at[pl.ds(0, NY * NZ * 144)], wd_r)
-    await_recv(grid_img.at[pl.ds(0, (NX - 1) * SLOT_ROWS)], gx_r.at[0])
+    image_wait(0)
     multiply(h)
     q_step(2, (1,))
     q_step(6, (1,))
-    await_recv(grid_img.at[pl.ds(0, (NX - 1) * SLOT_ROWS)], gx_r.at[1])
+    image_wait(1)
     multiply(1 - h)
 
     column = lax.broadcasted_iota(jnp.int32, (GRID, 128), 0)
@@ -293,16 +331,32 @@
             total = total + product(9, row_y) + value / (1.0 + jnp.exp(-value))
         fs_ref[pl.ds((gy // 2) * GRID, GRID), :] = total
     mean = (fs_ref[pl.ds(0, 144, stride=2), :] + fs_ref[pl.ds(1, 144, stride=2), :]) * 0.25
-    own_pool = pooled.at[c, my_slot]
     own_pool[...] = mean.astype(jnp.bfloat16)
 
-    remote(own_pool, own_pool, pool_s, oz_r, flip).start()
-    to_x(own_pool, pool_s, ox_r)
+    def pool_to_x(piece, dst):
+        for k in range(1, NX):
+            remote(piece, dst, pool_s, ox_r, me.at(x=plus(x, k, NX), c=1)).start()
+
+    remote(own_pool, pooled.at[c, my_slot], pool_s, oz_r.at[c], me.at(h=1 - h, c=1)).start()
+    pool_to_x(own_pool, pooled.at[c, my_slot])
+
+    @pl.when(c == 0)
+    def _():
+        remote(own_pool, pooled.at[0, my_slot], pool_cs, oc_r, sibling).start()
+
+    @pl.when(c == 1)
+    def _():
+        pooled[1, my_slot] = own_pool[...]
+
     for m in (1, 5, 3, 7):
         q_step(m, ())
-    flip_pool = pooled.at[c, flip_slot]
-    await_recv(flip_pool, oz_r)
-    to_x(flip_pool, pool_s, ox_r)
+    @pl.when(c == 1)
+    def _():
+        for i in (1, 0):
+            flip_pool = pooled.at[i, flip_slot]
+            await_recv(flip_pool, oz_r.at[i])
+            pool_to_x(flip_pool, flip_pool)
+
     await_recv(proj_cols.at[pl.ds(0, (NY - 1) * NZ)], qy_r)
 
     for t in range(4 * NX):
@@ -310,34 +364,50 @@
         proj_perm[pl.ds(t * 64, 32), :] = proj_cols[2 * block]
         proj_perm[pl.ds(t * 64 + 32, 32), :] = proj_cols[2 * block + 1]
 
-    await_recv(pooled.at[c, pl.ds(0, 2 * (NX - 1))], ox_r)
-    remote(pooled.at[c], pooled.at[c], pool_cs, od_r, sibling).start()
-    await_recv(pooled.at[other], od_r)
+    @pl.when(c == 1)
+    def _():
+        await_recv(pooled.at[0, my_slot], oc_r)
+        await_recv(pooled.at[:, pl.ds(0, 2 * (NX - 1))], ox_r)
+        remote(pooled, pooled, pool_cs, od_r, sibling).start()
+
+    @pl.when(c == 0)
+    def _():
+        await_recv(pooled, od_r)
+
+    def project(img):
+        lhs = jnp.concatenate([pooled[img, s] for s in range(SLOTS)], axis=1)
+        return jnp.dot(lhs, proj_perm[...], preferred_element_type=jnp.float32).astype(jnp.bfloat16)
 
     results = []
     for slot in range(2):
-        index = slot_ref[slot]
-        lhs = jnp.concatenate([pooled[index, s] for s in range(SLOTS)], axis=1)
-        result[slot] = jnp.dot(lhs, proj_perm[...], preferred_element_type=jnp.float32).astype(jnp.bfloat16)
+        result[slot] = project(slot_ref[slot])
         results.append(pltpu.make_async_copy(result.at[slot], out_ref.at[slot], loc.at[slot]))
         results[-1].start()
 
     ce_conv.wait_send()
     ce_img.wait_send()
     await_send(weights.at[pl.ds(0, (NZ - 1 + (NY - 1) * NZ + NY * NZ) * 144)], w_s)
-    await_send(grid_img.at[pl.ds(0, (2 * (NX - 1) + 1) * SLOT_ROWS)], img_s)
+    await_send(grid_img.at[pl.ds(0, (2 * (NX - 1) + 1) * BODY_ROWS)], img_s)
+    await_send(rests.at[pl.ds(0, 2 * (NX - 1) + 1)], rest_s)
     await_send(proj_all.at[c, pl.ds(0, 2 * (NX - 1) + 1)], proj_s)
     await_send(proj_all.at[c], proj_cs)
     await_send(proj_cols.at[pl.ds(0, NZ - 1 + (NY - 1) * NZ)], q_s)
-    await_send(pooled.at[c, pl.ds(0, 2 * (NX - 1) + 1)], pool_s)
-    await_send(pooled.at[c], pool_cs)
+    @pl.when(c == 0)
+    def _():
+        await_send(pooled.at[0, pl.ds(0, NX)], pool_s)
+        await_send(own_pool, pool_cs)
+
+    @pl.when(c == 1)
+    def _():
+        await_send(pooled.at[:, pl.ds(0, (3 * (NX - 1) + 1) // 2)], pool_s)
+        await_send(pooled, pool_cs)
+
     for copy in results:
         copy.wait()
 
 
 def per_device(patches, image_slot, trainer_blocks, conv_weight, proj_weight):
     dma = pltpu.SemaphoreType.DMA
-    smem = pl.BlockSpec(memory_space=pltpu.SMEM)
     anywhere = pl.BlockSpec(memory_space=pl.ANY)
     bf16, f32 = jnp.bfloat16, jnp.float32
     sems = [
@@ -349,6 +419,7 @@
         dma,
         dma,
         dma,
+        dma,
         dma((2,)),
         dma((NZ - 1,)),
         dma((2 * (NY - 1),)),
@@ -356,10 +427,13 @@
         dma((len(CUTS),)),
         dma((2,)),
         dma,
+        dma((2,)),
+        dma,
         dma,
         dma,
         dma((NZ - 1,)),
         dma,
+        dma((2,)),
         dma,
         dma,
         dma,
@@ -367,12 +441,16 @@
     return pl.pallas_call(
         kernel,
         out_shape=jax.ShapeDtypeStruct((2, 144, 512), bf16),
-        in_specs=[smem, smem, anywhere, anywhere, anywhere],
+        in_specs=[pl.BlockSpec(memory_space=pltpu.HBM)] * 5,
         out_specs=anywhere,
         scratch_shapes=[
-            pltpu.VMEM((2, 36, 1024), bf16),
-            pltpu.VMEM((2, 144, 64), bf16),
+            pltpu.SMEM((16,), jnp.int32),
+            pltpu.SMEM((2,), jnp.int32),
+            pltpu.VMEM((2, 36, 2, 1024), bf16),
+            pltpu.VMEM((2, 64, 288), bf16),
+            pltpu.VMEM((288, 128), bf16),
             pltpu.VMEM((SLOTS * SLOT_ROWS, 1024), bf16),
+            pltpu.VMEM((SLOTS, 16, 512), bf16),
             pltpu.VMEM((10 * 1024, 128), bf16),
             pltpu.VMEM((10, SLOTS * SLOT_ROWS, 128), f32),
             pltpu.VMEM((288, 128), f32),
@@ -380,8 +458,9 @@
             pltpu.VMEM((2, SLOTS, 32, 512), bf16),
             pltpu.VMEM((NY * NZ, 32, 512), bf16),
             pltpu.VMEM((1024, 512), bf16),
+            pltpu.VMEM((144, 128), bf16),
             pltpu.VMEM((2, 144, 512), bf16),
-            dma((3,)),
+            dma((5,)),
         ]
         + sems,
         compiler_params=pltpu.CompilerParams(
@@ -389,7 +468,7 @@
         ),
         cost_estimate=pl.CostEstimate(flops=2_000_000_000, bytes_accessed=600_000, transcendentals=73728),
         name="vision",
-    )(trainer_blocks, image_slot, patches, conv_weight, proj_weight)
+    )(*(pltpu.with_memory_space_constraint(a, pltpu.HBM) for a in (trainer_blocks, image_slot, jnp.transpose(patches, (1, 0, 2)), conv_weight.T, proj_weight)))
 
 
 def solution(mesh):

time: 71.1 us -> 66.8 us (0.940)
  the two profiles are of different devices: /device:TPU:1 before, /device:TPU:16 now
where the time goes in v4:
time: 66.8 us; the launch traced here: 66.7 us
  Pallas kernels  65.9 us (99%)
  local copies, waits for them, and re-layouts  0.72 us (1%)
    pallas_call x1, Pallas kernels, per_device(): pl.pallas_call(kernel, out_shape=jax.ShapeDtypeStruct((2, 144, 512), bf16...  65.9 us

profile of v4, /device:TPU:16, one launch (start us, length us, event | category | flops | bytes accessed | tf_op | source)
XLA Modules:
  0.0 66.7 jit_solution(8888227685941020776)
XLA Ops:
  0.0 65.9 %vision.1 = bf16[2,144,512]{2,1,0:T(8,128)(2,1)S(1)} custom-call(s32[16]{0:T(128)} %tb_in.1, s32[2]{0:T(128)} %slot_in.1, bf16[36,2,1024]{2,1,0:T(2,128)(2,1)} %bitcast.2, bf16[64,288]{1,0:T(8,128)(2,1)} %bitcast.3, bf16[32,512]{1,0:T(8,128)(2,1)} %proj.1), custom_call_target="tpu_custom_call" | custom-call | flops 2000000000 | bytes 600000 | tf_op jit(solution)/shard_map/vision/pallas_call | solution.py:441
  66.0 0.7 %copy.7 = bf16[2,144,512]{2,1,0:T(8,128)(2,1)} copy(bf16[2,144,512]{2,1,0:T(8,128)(2,1)S(1)} %vision.1) | data formatting | bytes 589824

commit v5 on v4

--- a/solution.py
+++ b/solution.py
@@ -69,6 +69,8 @@
     proj_perm,
     own_pool,
     result,
+    half_ok,
+    flip_ok,
     loc,
     ce_s,
     w_s,
@@ -125,16 +127,18 @@
     def greet(where):
         pl.semaphore_signal(barrier, inc=1, device_id=where, device_id_type=MESH)
 
-    greet(flip)
-    greet(me.at(h=1 - h, c=other))
     for k in range(1, NZ):
-        greet(me.at(z=plus(z, k, NZ)))
+        greet(me.at(z=plus(z, k, NZ), c=1))
     for k in range(1, NX):
-        greet(me.at(x=plus(x, k, NX)))
-        greet(me.at(x=plus(x, k, NX), c=other))
+        greet(me.at(x=plus(x, k, NX), c=1))
     for k in range(1, NY):
-        greet(me.at(y=plus(y, k, NY)))
-    greet(sibling)
+        greet(me.at(y=plus(y, k, NY), c=1))
+
+    @pl.when(c == 0)
+    def _():
+        greet(sibling)
+
+    greet(me.at(h=1 - h, c=0))
 
     local = [
         pltpu.make_async_copy(patches, tokens.at[c], loc.at[0]),
@@ -148,7 +152,25 @@
 
     for copy in local:
         copy.wait()
-    pl.semaphore_wait(barrier, 2 + (NZ - 1) + 2 * (NX - 1) + (NY - 1) + 1)
+    @pl.when(c == 1)
+    def _():
+        pl.semaphore_wait(barrier, 2 * (NZ - 1 + NX - 1 + NY - 1) + 1)
+        pl.semaphore_signal(half_ok, inc=1, device_id=sibling, device_id_type=MESH)
+
+    @pl.when(c == 0)
+    def _():
+        pl.semaphore_wait(half_ok, 1)
+
+    def meet_other_half():
+        @pl.when(c == 0)
+        def _():
+            pl.semaphore_wait(barrier, 2)
+            pl.semaphore_signal(flip_ok, inc=1, device_id=sibling, device_id_type=MESH)
+
+        @pl.when(c == 1)
+        def _():
+            pl.semaphore_wait(flip_ok, 1)
+
 
     ce_conv = remote(halves.at[c], halves.at[c], ce_s.at[0], ce_r.at[0], sibling)
     ce_conv.start()
@@ -204,8 +226,13 @@
     pair_rows[...] = both.T[:288].astype(jnp.bfloat16)
     own_shard[...] = pair_rows[pl.ds(pl.multiple_of(c * 144, 16), 144), :]
     w_step(0, (4, 2, 1))
-    remote(own_proj, own_proj, proj_s, pz_r, flip).start()
     to_x(own_proj, proj_s, px_r)
+
+    @pl.when(h == 1)
+    def _():
+        meet_other_half()
+        remote(own_proj, own_proj, proj_s, pz_r, flip).start()
+
 
     await_recv(tokens.at[other], ce_r.at[1])
     mine = [
@@ -266,7 +293,6 @@
             z_ref[2 * n, rows, :] = prod[:, :128]
             z_ref[2 * n + 1, rows, :] = prod[:, 128:]
 
-    flip_cut(0)
     row = lax.broadcasted_iota(jnp.int32, (1024, 128), 0)
     lane = lax.broadcasted_iota(jnp.int32, (1024, 128), 1)
     first = tb_ref[2 * my_slot] * 64
@@ -274,10 +300,25 @@
     wanted = lane + jnp.where(lane < 64, first, second)
     weights[pl.ds(9 * 1024, 1024), :] = jnp.where(row == wanted, 1.0, 0.0).astype(jnp.bfloat16)
     w_step(4, (2, 1))
-    flip_cut(1)
-    flip_rest()
+    @pl.when(h == 1)
+    def _():
+        flip_cut(0)
+
+    @pl.when(h == 0)
+    def _():
+        meet_other_half()
+        remote(own_proj, own_proj, proj_s, pz_r, flip).start()
+        flip_cut(0)
+        flip_cut(1)
+        flip_rest()
+
     w_step(2, (1,))
     w_step(6, (1,))
+    @pl.when(h == 1)
+    def _():
+        flip_cut(1)
+        flip_rest()
+
     await_recv(flip_proj, pz_r)
     to_x(flip_proj, proj_s, px_r)
     w_step(1, ())
@@ -300,12 +341,22 @@
     rest_step()
     for j in range(1, NY):
         w_rest(j, 1)
-    q_step(4, (2, 1))
+    @pl.when(h == 0)
+    def _():
+        q_step(4, (2, 1))
+
     await_recv(weights.at[pl.ds(0, NY * NZ * 144)], wd_r)
     image_wait(0)
     multiply(h)
-    q_step(2, (1,))
-    q_step(6, (1,))
+    @pl.when(h == 0)
+    def _():
+        q_step(2, (1,))
+        q_step(6, (1,))
+
+    @pl.when(h == 1)
+    def _():
+        q_step(4, (2, 1))
+
     image_wait(1)
     multiply(1 - h)
 
@@ -347,6 +398,11 @@
     @pl.when(c == 1)
     def _():
         pooled[1, my_slot] = own_pool[...]
+
+    @pl.when(h == 1)
+    def _():
+        q_step(2, (1,))
+        q_step(6, (1,))
 
     for m in (1, 5, 3, 7):
         q_step(m, ())
@@ -460,6 +516,8 @@
             pltpu.VMEM((1024, 512), bf16),
             pltpu.VMEM((144, 128), bf16),
             pltpu.VMEM((2, 144, 512), bf16),
+            pltpu.SemaphoreType.REGULAR,
+            pltpu.SemaphoreType.REGULAR,
             dma((5,)),
         ]
         + sems,

time: 66.8 us -> 64.4 us (0.964)
  the two profiles are of different devices: /device:TPU:16 before, /device:TPU:128 now
where the time goes in v5:
time: 64.4 us; the launch traced here: 64.3 us
  Pallas kernels  63.5 us (99%)
  local copies, waits for them, and re-layouts  0.72 us (1%)
    pallas_call x1, Pallas kernels, per_device(): pl.pallas_call(kernel, out_shape=jax.ShapeDtypeStruct((2, 144, 512), bf16...  63.5 us

profile of v5, /device:TPU:128, one launch (start us, length us, event | category | flops | bytes accessed | tf_op | source)
XLA Modules:
  0.0 64.3 jit_solution(5863866860759060793)
XLA Ops:
  0.0 63.5 %vision.1 = bf16[2,144,512]{2,1,0:T(8,128)(2,1)S(1)} custom-call(s32[16]{0:T(128)} %tb_in.1, s32[2]{0:T(128)} %slot_in.1, bf16[36,2,1024]{2,1,0:T(2,128)(2,1)} %bitcast.2, bf16[64,288]{1,0:T(8,128)(2,1)} %bitcast.3, bf16[32,512]{1,0:T(8,128)(2,1)} %proj.1), custom_call_target="tpu_custom_call" | custom-call | flops 2000000000 | bytes 600000 | tf_op jit(solution)/shard_map/vision/pallas_call | solution.py:497
  63.5 0.7 %copy.7 = bf16[2,144,512]{2,1,0:T(8,128)(2,1)} copy(bf16[2,144,512]{2,1,0:T(8,128)(2,1)S(1)} %vision.1) | data formatting | bytes 589824

commit v6 on v5

--- a/solution.py
+++ b/solution.py
@@ -68,6 +68,7 @@
     proj_cols,
     proj_perm,
     own_pool,
+    by_image,
     result,
     half_ok,
     flip_ok,
@@ -219,6 +220,22 @@
         for j in range(1, NY):
             remote(q_piece(m), q_piece(m), q_s, qy_r, me.at(y=plus(y, j, NY))).start()
 
+    def proj_along_x():
+        await_recv(flip_proj, pz_r)
+        to_x(flip_proj, proj_s, px_r)
+
+    def proj_to_sibling():
+        await_recv(proj_all.at[c, pl.ds(0, 2 * (NX - 1))], px_r)
+        remote(proj_all.at[c], proj_all.at[c], proj_cs, pd_r, sibling).start()
+
+    def proj_select():
+        await_recv(proj_all.at[other], pd_r)
+        holder = jnp.int32(0)
+        for t in range(4 * NX):
+            holder = jnp.where(tb_ref[t] == me.t, t, holder)
+        q_piece(0)[...] = proj_all[lax.rem(holder, 2), holder // 2]
+        q_step(0, (4, 2, 1))
+
     await_recv(halves.at[other], ce_r.at[0])
     own_shard = w_piece(0)
     both = jnp.concatenate([halves[0], halves[1]], axis=0).astype(jnp.float32)
@@ -293,6 +310,11 @@
             z_ref[2 * n, rows, :] = prod[:, :128]
             z_ref[2 * n + 1, rows, :] = prod[:, 128:]
 
+    @pl.when(h == 0)
+    def _():
+        meet_other_half()
+        remote(own_proj, own_proj, proj_s, pz_r, flip).start()
+
     row = lax.broadcasted_iota(jnp.int32, (1024, 128), 0)
     lane = lax.broadcasted_iota(jnp.int32, (1024, 128), 1)
     first = tb_ref[2 * my_slot] * 64
@@ -306,8 +328,6 @@
 
     @pl.when(h == 0)
     def _():
-        meet_other_half()
-        remote(own_proj, own_proj, proj_s, pz_r, flip).start()
         flip_cut(0)
         flip_cut(1)
         flip_rest()
@@ -319,20 +339,13 @@
         flip_cut(1)
         flip_rest()
 
-    await_recv(flip_proj, pz_r)
-    to_x(flip_proj, proj_s, px_r)
+    proj_along_x()
     w_step(1, ())
     w_step(5, ())
-    await_recv(proj_all.at[c, pl.ds(0, 2 * (NX - 1))], px_r)
-    remote(proj_all.at[c], proj_all.at[c], proj_cs, pd_r, sibling).start()
+    proj_to_sibling()
     w_step(3, ())
     w_step(7, ())
-    await_recv(proj_all.at[other], pd_r)
-    holder = jnp.int32(0)
-    for t in range(4 * NX):
-        holder = jnp.where(tb_ref[t] == me.t, t, holder)
-    q_piece(0)[...] = proj_all[lax.rem(holder, 2), holder // 2]
-    q_step(0, (4, 2, 1))
+    proj_select()
 
     image_step(0)
     for j in range(1, NY):
@@ -384,12 +397,12 @@
     mean = (fs_ref[pl.ds(0, 144, stride=2), :] + fs_ref[pl.ds(1, 144, stride=2), :]) * 0.25
     own_pool[...] = mean.astype(jnp.bfloat16)
 
-    def pool_to_x(piece, dst):
+    def pool_to_x(piece, dst, half):
         for k in range(1, NX):
-            remote(piece, dst, pool_s, ox_r, me.at(x=plus(x, k, NX), c=1)).start()
+            remote(piece, dst, pool_s, ox_r.at[half], me.at(x=plus(x, k, NX), c=1)).start()
 
     remote(own_pool, pooled.at[c, my_slot], pool_s, oz_r.at[c], me.at(h=1 - h, c=1)).start()
-    pool_to_x(own_pool, pooled.at[c, my_slot])
+    pool_to_x(own_pool, pooled.at[c, my_slot], 0)
 
     @pl.when(c == 0)
     def _():
@@ -411,7 +424,19 @@
         for i in (1, 0):
             flip_pool = pooled.at[i, flip_slot]
             await_recv(flip_pool, oz_r.at[i])
-            pool_to_x(flip_pool, flip_pool)
+            pool_to_x(flip_pool, flip_pool, 1)
+
+    def pool_of_half(half):
+        return pooled.at[:, pl.ds((h if half == 0 else 1 - h) * NX, NX)]
+
+    def pool_to_first(half):
+        await_recv(pooled.at[:, pl.ds(0, NX - 1)], ox_r.at[half])
+        remote(pool_of_half(half), pool_of_half(half), pool_cs, od_r.at[half], sibling).start()
+
+    @pl.when(c == 1)
+    def _():
+        await_recv(pooled.at[0, my_slot], oc_r)
+        pool_to_first(0)
 
     await_recv(proj_cols.at[pl.ds(0, (NY - 1) * NZ)], qy_r)
 
@@ -420,23 +445,35 @@
         proj_perm[pl.ds(t * 64, 32), :] = proj_cols[2 * block]
         proj_perm[pl.ds(t * 64 + 32, 32), :] = proj_cols[2 * block + 1]
 
+    @pl.when(c == 0)
+    def _():
+        await_recv(pool_of_half(0), od_r.at[0])
+
+    def project(half):
+        first = (h if half == 0 else 1 - h) * NX
+        rows = pl.ds(pl.multiple_of(first * 128, 512), 512)
+        lhs = jnp.concatenate(
+            [jnp.concatenate([pooled[i, first + s] for s in range(NX)], axis=1) for i in range(2)], axis=0
+        )
+        return jnp.dot(lhs, proj_perm[rows, :], preferred_element_type=jnp.float32)
+
+    half_sum = project(0)
+    for i in range(2):
+        by_image[i] = half_sum[144 * i : 144 * (i + 1)]
     @pl.when(c == 1)
     def _():
-        await_recv(pooled.at[0, my_slot], oc_r)
-        await_recv(pooled.at[:, pl.ds(0, 2 * (NX - 1))], ox_r)
-        remote(pooled, pooled, pool_cs, od_r, sibling).start()
+        pool_to_first(1)
 
     @pl.when(c == 0)
     def _():
-        await_recv(pooled, od_r)
-
-    def project(img):
-        lhs = jnp.concatenate([pooled[img, s] for s in range(SLOTS)], axis=1)
-        return jnp.dot(lhs, proj_perm[...], preferred_element_type=jnp.float32).astype(jnp.bfloat16)
-
+        await_recv(pool_of_half(1), od_r.at[1])
+
+    half_sum = project(1)
+    for i in range(2):
+        by_image[i] += half_sum[144 * i : 144 * (i + 1)]
     results = []
     for slot in range(2):
-        result[slot] = project(slot_ref[slot])
+        result[slot] = by_image[slot_ref[slot]].astype(jnp.bfloat16)
         results.append(pltpu.make_async_copy(result.at[slot], out_ref.at[slot], loc.at[slot]))
         results[-1].start()
 
@@ -490,9 +527,9 @@
         dma((NZ - 1,)),
         dma,
         dma((2,)),
-        dma,
-        dma,
-        dma,
+        dma((2,)),
+        dma,
+        dma((2,)),
     ]
     return pl.pallas_call(
         kernel,
@@ -515,6 +552,7 @@
             pltpu.VMEM((NY * NZ, 32, 512), bf16),
             pltpu.VMEM((1024, 512), bf16),
             pltpu.VMEM((144, 128), bf16),
+            pltpu.VMEM((2, 144, 512), f32),
             pltpu.VMEM((2, 144, 512), bf16),
             pltpu.SemaphoreType.REGULAR,
             pltpu.SemaphoreType.REGULAR,

time: 64.4 us -> 61.1 us (0.949)
  the two profiles are of different devices: /device:TPU:128 before, /device:TPU:1 now
where the time goes in v6:
time: 61.1 us; the launch traced here: 61 us
  Pallas kernels  60.2 us (99%)
  local copies, waits for them, and re-layouts  0.72 us (1%)
    pallas_call x1, Pallas kernels, per_device(): pl.pallas_call(kernel, out_shape=jax.ShapeDtypeStruct((2, 144, 512), bf16...  60.2 us

profile of v6, /device:TPU:1, one launch (start us, length us, event | category | flops | bytes accessed | tf_op | source)
XLA Modules:
  0.0 61.0 jit_solution(1951564585209868882)
XLA Ops:
  0.0 60.2 %vision.1 = bf16[2,144,512]{2,1,0:T(8,128)(2,1)S(1)} custom-call(s32[16]{0:T(128)} %tb_in.1, s32[2]{0:T(128)} %slot_in.1, bf16[36,2,1024]{2,1,0:T(2,128)(2,1)} %bitcast.2, bf16[64,288]{1,0:T(8,128)(2,1)} %bitcast.3, bf16[32,512]{1,0:T(8,128)(2,1)} %proj.1), custom_call_target="tpu_custom_call" | custom-call | flops 2000000000 | bytes 600000 | tf_op jit(solution)/shard_map/vision/pallas_call | solution.py:534
  60.2 0.7 %copy.7 = bf16[2,144,512]{2,1,0:T(8,128)(2,1)} copy(bf16[2,144,512]{2,1,0:T(8,128)(2,1)S(1)} %vision.1) | data formatting | bytes 589824

commit v7 on v6

--- a/solution.py
+++ b/solution.py
@@ -234,7 +234,6 @@
         for t in range(4 * NX):
             holder = jnp.where(tb_ref[t] == me.t, t, holder)
         q_piece(0)[...] = proj_all[lax.rem(holder, 2), holder // 2]
-        q_step(0, (4, 2, 1))
 
     await_recv(halves.at[other], ce_r.at[0])
     own_shard = w_piece(0)
@@ -343,34 +342,44 @@
     w_step(1, ())
     w_step(5, ())
     proj_to_sibling()
+    @pl.when(h == 0)
+    def _():
+        proj_select()
+        q_step(0, (4, 1, 2, 3))
+
     w_step(3, ())
     w_step(7, ())
-    proj_select()
+    @pl.when(h == 1)
+    def _():
+        proj_select()
+        q_step(0, (4, 2, 1))
+
 
     image_step(0)
     for j in range(1, NY):
         w_rest(j, 0)
     image_step(1)
     rest_step()
+    @pl.when(h == 0)
+    def _():
+        q_step(4, (1, 2, 3))
+
+    @pl.when(h == 0)
+    def _():
+        for m in (1, 2, 3):
+            q_step(m, ())
+
     for j in range(1, NY):
         w_rest(j, 1)
-    @pl.when(h == 0)
-    def _():
-        q_step(4, (2, 1))
-
     await_recv(weights.at[pl.ds(0, NY * NZ * 144)], wd_r)
     image_wait(0)
     multiply(h)
+    image_wait(1)
     @pl.when(h == 0)
     def _():
-        q_step(2, (1,))
-        q_step(6, (1,))
-
-    @pl.when(h == 1)
-    def _():
-        q_step(4, (2, 1))
-
-    image_wait(1)
+        for m in (5, 6, 7):
+            q_step(m, ())
+
     multiply(1 - h)
 
     column = lax.broadcasted_iota(jnp.int32, (GRID, 128), 0)
@@ -414,11 +423,18 @@
 
     @pl.when(h == 1)
     def _():
+        q_step(4, (2, 1))
+
+    @pl.when(h == 1)
+    def _():
         q_step(2, (1,))
         q_step(6, (1,))
 
-    for m in (1, 5, 3, 7):
-        q_step(m, ())
+    @pl.when(h == 1)
+    def _():
+        for m in (1, 5, 3, 7):
+            q_step(m, ())
+
     @pl.when(c == 1)
     def _():
         for i in (1, 0):

time: 61.1 us -> 60.6 us (level)
  the two profiles are of different devices: /device:TPU:1 before, /device:TPU:32 now
where the time goes in v7:
time: 60.6 us; the launch traced here: 60.4 us
  Pallas kernels  59.7 us (99%)
  local copies, waits for them, and re-layouts  0.72 us (1%)
    pallas_call x1, Pallas kernels, per_device(): pl.pallas_call(kernel, out_shape=jax.ShapeDtypeStruct((2, 144, 512), bf16...  59.7 us

profile of v7, /device:TPU:32, one launch (start us, length us, event | category | flops | bytes accessed | tf_op | source)
XLA Modules:
  0.0 60.4 jit_solution(2195249096750944680)
XLA Ops:
  0.0 59.7 %vision.1 = bf16[2,144,512]{2,1,0:T(8,128)(2,1)S(1)} custom-call(s32[16]{0:T(128)} %tb_in.1, s32[2]{0:T(128)} %slot_in.1, bf16[36,2,1024]{2,1,0:T(2,128)(2,1)} %bitcast.2, bf16[64,288]{1,0:T(8,128)(2,1)} %bitcast.3, bf16[32,512]{1,0:T(8,128)(2,1)} %proj.1), custom_call_target="tpu_custom_call" | custom-call | flops 2000000000 | bytes 600000 | tf_op jit(solution)/shard_map/vision/pallas_call | solution.py:550
  59.7 0.7 %copy.7 = bf16[2,144,512]{2,1,0:T(8,128)(2,1)} copy(bf16[2,144,512]{2,1,0:T(8,128)(2,1)S(1)} %vision.1) | data formatting | bytes 589824

commit v8 on v7

--- a/solution.py
+++ b/solution.py
@@ -347,6 +347,10 @@
         proj_select()
         q_step(0, (4, 1, 2, 3))
 
+    @pl.when(h == 1)
+    def _():
+        image_step(0)
+
     w_step(3, ())
     w_step(7, ())
     @pl.when(h == 1)
@@ -355,7 +359,10 @@
         q_step(0, (4, 2, 1))
 
 
-    image_step(0)
+    @pl.when(h == 0)
+    def _():
+        image_step(0)
+
     for j in range(1, NY):
         w_rest(j, 0)
     image_step(1)

time: 60.6 us -> 59.8 us (0.987)
  the two profiles are of different devices: /device:TPU:32 before, /device:TPU:1 now
where the time goes in v8:
time: 59.8 us; the launch traced here: 58.8 us
  Pallas kernels  58.1 us (97%)
  local copies, waits for them, and re-layouts  0.72 us (1%)
    pallas_call x1, Pallas kernels, per_device(): pl.pallas_call(kernel, out_shape=jax.ShapeDtypeStruct((2, 144, 512), bf16...  58.1 us

profile of v8, /device:TPU:1, one launch (start us, length us, event | category | flops | bytes accessed | tf_op | source)
XLA Modules:
  0.0 58.8 jit_solution(14045725286148663779)
XLA Ops:
  0.0 58.1 %vision.1 = bf16[2,144,512]{2,1,0:T(8,128)(2,1)S(1)} custom-call(s32[16]{0:T(128)} %tb_in.1, s32[2]{0:T(128)} %slot_in.1, bf16[36,2,1024]{2,1,0:T(2,128)(2,1)} %bitcast.2, bf16[64,288]{1,0:T(8,128)(2,1)} %bitcast.3, bf16[32,512]{1,0:T(8,128)(2,1)} %proj.1), custom_call_target="tpu_custom_call" | custom-call | flops 2000000000 | bytes 600000 | tf_op jit(solution)/shard_map/vision/pallas_call | solution.py:557
  58.1 0.7 %copy.7 = bf16[2,144,512]{2,1,0:T(8,128)(2,1)} copy(bf16[2,144,512]{2,1,0:T(8,128)(2,1)S(1)} %vision.1) | data formatting | bytes 589824

commit v9 on v8

--- a/solution.py
+++ b/solution.py
@@ -569,7 +569,7 @@
             pltpu.VMEM((SLOTS, 16, 512), bf16),
             pltpu.VMEM((10 * 1024, 128), bf16),
             pltpu.VMEM((10, SLOTS * SLOT_ROWS, 128), f32),
-            pltpu.VMEM((288, 128), f32),
+            pltpu.VMEM((296, 128), f32),
             pltpu.VMEM((2, SLOTS, 144, 128), bf16),
             pltpu.VMEM((2, SLOTS, 32, 512), bf16),
             pltpu.VMEM((NY * NZ, 32, 512), bf16),

time: 59.8 us -> 59.8 us (level)
  no operation moved by 1% of the time
where the time goes in v9:
time: 59.8 us; the launch traced here: 58.8 us
  Pallas kernels  58.1 us (97%)
  local copies, waits for them, and re-layouts  0.72 us (1%)
    pallas_call x1, Pallas kernels, per_device(): pl.pallas_call(kernel, out_shape=jax.ShapeDtypeStruct((2, 144, 512), bf16...  58.1 us

profile of v9, /device:TPU:1, one launch (start us, length us, event | category | flops | bytes accessed | tf_op | source)
XLA Modules:
  0.0 58.8 jit_solution(107729076251140979)
XLA Ops:
  0.0 58.1 %vision.1 = bf16[2,144,512]{2,1,0:T(8,128)(2,1)S(1)} custom-call(s32[16]{0:T(128)} %tb_in.1, s32[2]{0:T(128)} %slot_in.1, bf16[36,2,1024]{2,1,0:T(2,128)(2,1)} %bitcast.2, bf16[64,288]{1,0:T(8,128)(2,1)} %bitcast.3, bf16[32,512]{1,0:T(8,128)(2,1)} %proj.1), custom_call_target="tpu_custom_call" | custom-call | flops 2000000000 | bytes 600000 | tf_op jit(solution)/shard_map/vision/pallas_call | solution.py:557
  58.1 0.7 %copy.7 = bf16[2,144,512]{2,1,0:T(8,128)(2,1)} copy(bf16[2,144,512]{2,1,0:T(8,128)(2,1)S(1)} %vision.1) | data formatting | bytes 589824

commit v10 on v9

--- a/solution.py
+++ b/solution.py
@@ -69,6 +69,7 @@
     proj_perm,
     own_pool,
     by_image,
+    rounded,
     result,
     half_ok,
     flip_ok,
@@ -493,10 +494,10 @@
 
     half_sum = project(1)
     for i in range(2):
-        by_image[i] += half_sum[144 * i : 144 * (i + 1)]
+        rounded[i] = (by_image[i] + half_sum[144 * i : 144 * (i + 1)]).astype(jnp.bfloat16)
     results = []
     for slot in range(2):
-        result[slot] = by_image[slot_ref[slot]].astype(jnp.bfloat16)
+        result[slot] = rounded[slot_ref[slot]]
         results.append(pltpu.make_async_copy(result.at[slot], out_ref.at[slot], loc.at[slot]))
         results[-1].start()
 
@@ -577,6 +578,7 @@
             pltpu.VMEM((144, 128), bf16),
             pltpu.VMEM((2, 144, 512), f32),
             pltpu.VMEM((2, 144, 512), bf16),
+            pltpu.VMEM((2, 144, 512), bf16),
             pltpu.SemaphoreType.REGULAR,
             pltpu.SemaphoreType.REGULAR,
             dma((5,)),

time: 59.8 us -> 59.8 us (level)
  no operation moved by 1% of the time
where the time goes in v10:
time: 59.8 us; the launch traced here: 58.8 us
  Pallas kernels  58.1 us (97%)
  local copies, waits for them, and re-layouts  0.72 us (1%)
    pallas_call x1, Pallas kernels, per_device(): pl.pallas_call(kernel, out_shape=jax.ShapeDtypeStruct((2, 144, 512), bf16...  58.1 us

profile of v10, /device:TPU:1, one launch (start us, length us, event | category | flops | bytes accessed | tf_op | source)
XLA Modules:
  0.0 58.8 jit_solution(16235338320179198080)
XLA Ops:
  0.0 58.1 %vision.1 = bf16[2,144,512]{2,1,0:T(8,128)(2,1)S(1)} custom-call(s32[16]{0:T(128)} %tb_in.1, s32[2]{0:T(128)} %slot_in.1, bf16[36,2,1024]{2,1,0:T(2,128)(2,1)} %bitcast.2, bf16[64,288]{1,0:T(8,128)(2,1)} %bitcast.3, bf16[32,512]{1,0:T(8,128)(2,1)} %proj.1), custom_call_target="tpu_custom_call" | custom-call | flops 2000000000 | bytes 600000 | tf_op jit(solution)/shard_map/vision/pallas_call | solution.py:558
  58.1 0.7 %copy.7 = bf16[2,144,512]{2,1,0:T(8,128)(2,1)} copy(bf16[2,144,512]{2,1,0:T(8,128)(2,1)S(1)} %vision.1) | data formatting | bytes 589824
